TPU v7x, 512 devices: a whole 4x4x16 slice. The times are simulated.
512 devices in a mesh: gx: 16 (over z), gy: 4 (over x_lo, core), gz: 8 (over x_hi, y).
Axes of the slice: x: 4 (x_hi: 2, x_lo: 2; x = x_hi * 2 + x_lo), y: 4, z: 16, core: 2. Of those that a mesh axis runs over, the one named last changes fastest.
Arguments:
- fine_start: float32 [5, 32, 256, 512], P(None, 'gz', 'gx', 'gy'), as said below
- fine_section: float32 [5, 32, 256, 512], P(None, 'gz', 'gx', 'gy'), as said below
- fine_noise: float32 [3, 32, 256, 512], P(None, 'gz', 'gx', 'gy'), may hold values from -6 to 6
- coarse_start: float32 [5, 16, 128, 256], P(None, 'gz', 'gx', 'gy'), as said below
- coarse_section: float32 [5, 16, 128, 256], P(None, 'gz', 'gx', 'gy'), as said below
- kernel: float32 [3, 9], replicated, may hold values from -3 to 3
- owner: int32 [8], replicated, may hold values from 0 to 7, each once
Outputs:
- fine_next: float32 [5, 32, 256, 512], P(None, 'gz', 'gx', 'gy')
- coarse_next: float32 [5, 16, 128, 256], P(None, 'gz', 'gx', 'gy')
Inputs may be any that keep to these rules, and one draw needn't show every extreme that they name: owner is a permutation of 0 to 7. `fine_section`: density lies in [0.5, 2], each velocity component within [-1.2, 1.2], pressure (0.4 (E - |m|^2 / (2 rho))) in [0.4, 2]. `fine_start`: as for fine_section. `coarse_section`: as for fine_section. `coarse_start`: as for fine_section.
All inputs are finite; a program needn't handle non-finite values.
Results may differ from a plain program's by a relative error of at most 0.00005.
Values sent between devices are 32-bit elements; how exact they have to be, the bound alone decides.
A program may use at most 64 MiB of HBM per device.

v0:
```python
import jax
import jax.numpy as jnp
from jax import lax
from jax.sharding import PartitionSpec as P

GAMMA = 1.4
CFL_NUMBER = 0.4
WENO_EPS = 1e-06
RESTRICT_SCALE = 0.35355339059327373


def padded_2(cells, sides, width):
    for axis, dim in sides:
        count = lax.axis_size(axis)
        head = lax.slice_in_dim(cells, 0, width, axis=dim)
        tail = lax.slice_in_dim(cells, cells.shape[dim] - width, cells.shape[dim], axis=dim)
        cells = jnp.concatenate(
            [
                lax.ppermute(tail, axis, [(i, (i + 1) % count) for i in range(count)]),
                cells,
                lax.ppermute(head, axis, [((i + 1) % count, i) for i in range(count)]),
            ],
            axis=dim,
        )
    return cells


def flux_fields(state, component):
    density = state[0]
    velocity = state[component] / density
    pressure = (GAMMA - 1.0) * (
        state[4] - 0.5 * (state[1] * state[1] + state[2] * state[2] + state[3] * state[3]) / density
    )
    entries = [
        state[component],
        state[1] * velocity,
        state[2] * velocity,
        state[3] * velocity,
        (state[4] + pressure) * velocity,
    ]
    entries[component] = entries[component] + pressure
    return jnp.stack(entries)


def weno_side(first, second, third, fourth, fifth):
    cand_low = (2.0 * first - 7.0 * second + 11.0 * third) / 6.0
    cand_mid = (-second + 5.0 * third + 2.0 * fourth) / 6.0
    cand_high = (2.0 * third + 5.0 * fourth - fifth) / 6.0
    smooth_low = (
        13.0 / 12.0 * (first - 2.0 * second + third) ** 2
        + 0.25 * (first - 4.0 * second + 3.0 * third) ** 2
    )
    smooth_mid = 13.0 / 12.0 * (second - 2.0 * third + fourth) ** 2 + 0.25 * (second - fourth) ** 2
    smooth_high = (
        13.0 / 12.0 * (third - 2.0 * fourth + fifth) ** 2
        + 0.25 * (3.0 * third - 4.0 * fourth + fifth) ** 2
    )
    weight_low = 0.1 / (WENO_EPS + smooth_low) ** 2
    weight_mid = 0.6 / (WENO_EPS + smooth_mid) ** 2
    weight_high = 0.3 / (WENO_EPS + smooth_high) ** 2
    return (weight_low * cand_low + weight_mid * cand_mid + weight_high * cand_high) / (
        weight_low + weight_mid + weight_high
    )


def sweep(extended, direction, wave_speed):
    extent = extended.shape[direction] - 6
    component = {1: 3, 2: 1, 3: 2}[direction]
    fluxes = flux_fields(extended, component)
    upwind = 0.5 * (fluxes + wave_speed * extended)
    downwind = 0.5 * (fluxes - wave_speed * extended)

    def pick(values, start):
        return lax.slice_in_dim(values, start, start + extent + 1, axis=direction)

    face_flux = weno_side(
        pick(upwind, 0), pick(upwind, 1), pick(upwind, 2), pick(upwind, 3), pick(upwind, 4)
    )
    face_flux = face_flux + weno_side(
        pick(downwind, 5),
        pick(downwind, 4),
        pick(downwind, 3),
        pick(downwind, 2),
        pick(downwind, 1),
    )
    return lax.slice_in_dim(face_flux, 1, extent + 1, axis=direction) - lax.slice_in_dim(
        face_flux, 0, extent, axis=direction
    )


def wave_speed_of(state):
    density = state[0]
    pressure = (GAMMA - 1.0) * (
        state[4] - 0.5 * (state[1] * state[1] + state[2] * state[2] + state[3] * state[3]) / density
    )
    sound = jnp.sqrt(GAMMA * pressure / density)
    fastest = (
        jnp.maximum(jnp.maximum(jnp.abs(state[1]), jnp.abs(state[2])), jnp.abs(state[3])) / density
        + sound
    )
    return jnp.max(fastest)


def advance(start, section, div_z, div_x, div_y, forcing, wave_speed, factor):
    density = section[0]
    source = jnp.stack(
        [
            jnp.zeros_like(density),
            factor * density * forcing[0],
            factor * density * forcing[1],
            factor * density * forcing[2],
            factor * (section[1] * forcing[0] + section[2] * forcing[1] + section[3] * forcing[2]),
        ]
    )
    change = -(div_z + div_x + div_y) + source
    return 0.75 * start + 0.25 * (section + CFL_NUMBER / wave_speed * change)


def conv_along(extended, taps, direction):
    extent = extended.shape[direction] - 8
    total = taps[0] * lax.slice_in_dim(extended, 0, extent, axis=direction)
    for offset in range(1, 9):
        total = total + taps[offset] * lax.slice_in_dim(
            extended, offset, offset + extent, axis=direction
        )
    return total


def section_from_rims(start, padded, forcing, wave_speed, factor):
    div_z = sweep(padded[:, :, 3:-3, 3:-3], 1, wave_speed)
    div_x = sweep(padded[:, 3:-3, :, 3:-3], 2, wave_speed)
    div_y = sweep(padded[:, 3:-3, 3:-3, :], 3, wave_speed)
    return advance(
        start, padded[:, 3:-3, 3:-3, 3:-3], div_z, div_x, div_y, forcing, wave_speed, factor
    )


def local(fine_start, fine_section, fine_noise, coarse_start, coarse_section, kernel, owner):
    speed_fine, speed_coarse = lax.pmax(
        (wave_speed_of(fine_section), wave_speed_of(coarse_section)), ("gx", "gy", "gz")
    )
    fine_padded = padded_2(fine_section, (("gx", 2), ("gy", 3), ("gz", 1)), 3)
    noise_padded = padded_2(fine_noise, (("gx", 2), ("gy", 3), ("gz", 1)), 4)
    forcing_fine = conv_along(
        conv_along(conv_along(noise_padded, kernel[0], 2), kernel[1], 3), kernel[2], 1
    )
    fine_next = section_from_rims(fine_start, fine_padded, forcing_fine, speed_fine, 1.0)
    half_z = fine_noise.shape[1] // 2
    restricted = (
        fine_noise.reshape(
            3, half_z, 2, fine_noise.shape[2] // 2, 2, fine_noise.shape[3] // 2, 2
        ).sum(axis=(2, 4, 6))
        * RESTRICT_SCALE
    )
    coarse_padded = padded_2(coarse_section, (("gx", 2), ("gy", 3)), 3)
    state_column, gathered_noise = (
        lax.all_gather(coarse_padded, "gz", axis=1, tiled=True),
        lax.all_gather(restricted, "gz", axis=1, tiled=True),
    )
    column_rims = padded_2(gathered_noise, (("gx", 2), ("gy", 3)), 4)
    noise_column = conv_along(conv_along(column_rims, kernel[0], 2), kernel[1], 3)
    groups = lax.axis_size("gz")
    column_planes = groups * half_z
    index_here = lax.axis_index("gz")
    own_block = jnp.sum(
        jnp.arange(groups, dtype=jnp.int32) * (owner == index_here).astype(jnp.int32)
    )
    state_blocks = state_column.reshape((5, groups, half_z) + state_column.shape[2:])
    state_geo = jnp.take(state_blocks, owner, axis=1).reshape(state_column.shape)
    state_tiled = jnp.concatenate([state_geo, state_geo, state_geo], axis=1)
    noise_tiled = jnp.concatenate([noise_column, noise_column, noise_column], axis=1)
    base_plane = column_planes + own_block * half_z
    state_window = lax.dynamic_slice_in_dim(state_tiled, base_plane - 3, half_z + 6, axis=1)
    noise_window = lax.dynamic_slice_in_dim(noise_tiled, base_plane - 4, half_z + 8, axis=1)
    forcing_coarse = conv_along(noise_window, kernel[2], 1)
    coarse_next = section_from_rims(coarse_start, state_window, forcing_coarse, speed_coarse, 2.0)
    return (fine_next, coarse_next)


def solution(mesh):
    in_specs = (
        P(None, "gz", "gx", "gy"),
        P(None, "gz", "gx", "gy"),
        P(None, "gz", "gx", "gy"),
        P(None, "gz", "gx", "gy"),
        P(None, "gz", "gx", "gy"),
        P(),
        P(),
    )
    out_specs = (P(None, "gz", "gx", "gy"), P(None, "gz", "gx", "gy"))
    return jax.shard_map(local, mesh=mesh, in_specs=in_specs, out_specs=out_specs, check_vma=False)
```

profile of v0, /device:TPU:1, one launch (start us, length us, event | category | flops | bytes accessed | tf_op | source)
XLA Modules:
  0.0 334.3 jit_solution(6274643272408335369)
XLA Ops:
  1.5 12.0 %collective-permute-start.7 = (f32[3,4,4,128]{3,2,1,0:T(4,128)S(1)}, f32[3,4,4,128]{3,2,1,0:T(4,128)S(1)}, u32[]{:S(2)}, u32[]{:S(2)}) collective-permute-start(f32[3,4,4,128]{3,2,1,0:T(4,128)S(1)} %get-tuple-element.60), channel_id=1, source_target_pairs={{32,0},{64,32},{96,64},{128,96},{160,128},{192,160},{224,192},{256... | collective-permute-start | bytes 73736 | tf_op jit(solution)/shard_map/ppermute | solution.py:21
  16.3 4.6 %collective-permute-start.1 = (f32[5,4,3,128]{3,2,1,0:T(4,128)S(1)}, f32[5,4,3,128]{3,2,1,0:T(4,128)S(1)}, u32[]{:S(2)}, u32[]{:S(2)}) collective-permute-start(f32[5,4,3,128]{3,2,1,0:T(4,128)S(1)} %get-tuple-element.56), channel_id=1, source_target_pairs={{32,0},{64,32},{96,64},{128,96},{160,128},{192,160},{224,192},{256... | collective-permute-start | bytes 92168 | tf_op jit(solution)/shard_map/ppermute | solution.py:21
  23.7 3.4 %collective-permute-start.12 = (f32[5,2,3,64]{3,2,0,1:T(4,128)S(1)}, f32[5,2,3,64]{3,2,0,1:T(4,128)S(1)}, u32[]{:S(2)}, u32[]{:S(2)}) collective-permute-start(f32[5,2,3,64]{3,2,0,1:T(4,128)S(1)} %get-tuple-element.63), channel_id=1, source_target_pairs={{0,32},{32,64},{64,96},{96,128},{128,160},{160,192},{192,224},{224... | collective-permute-start | bytes 23048 | tf_op jit(solution)/shard_map/ppermute | solution.py:19
  33.7 8.4 %reshape.97 = f32[3,2,2,8,2,64,2]{6,5,4,3,2,1,0:T(8,128)} reshape(f32[3,4,16,128]{3,2,1,0:T(8,128)} %param.9) | data formatting | bytes 196608 | tf_op jit(solution)/shard_map/reshape | solution.py:150
  42.8 3.3 reduce_sum.19
  46.1 28.5 %all_gather.7 = f32[3,16,8,64]{3,2,0,1:T(8,128)S(1)} all-gather(f32[3,2,8,64]{3,2,0,1:T(8,128)S(1)} %copy.35), channel_id=1, replica_groups=mesh['gx'=16,'gy'=4,'gz'=8] {'gz'}, dimensions={1}, use_global_device_ids=true | all-gather | bytes 110592 | tf_op jit(solution)/shard_map/all_gather | solution.py:158
  74.8 10.3 %collective-permute-start.15 = (f32[5,2,14,3]{3,2,0,1:T(8,128)S(1)}, f32[5,2,14,3]{3,2,0,1:T(8,128)S(1)}, u32[]{:S(2)}, u32[]{:S(2)}) collective-permute-start(f32[5,2,14,3]{3,2,0,1:T(8,128)S(1)} %get-tuple-element.62), channel_id=1, source_target_pairs={{8,0},{16,8},{24,16},{0,24},{9,1},{17,9},{25,17},{1,25},{10,2},{18... | collective-permute-start | bytes 5048 | tf_op jit(solution)/shard_map/ppermute | solution.py:21
  87.6 101.4 %all-reduce = (f32[]{:T(128)}, f32[]{:T(128)}) all-reduce(f32[]{:T(128)} %fusion.65, f32[]{:T(128)} %fusion.81), channel_id=1, replica_groups=mesh['gx'=16,'gy'=4,'gz'=8] {'gx','gy','gz'}, use_global_device_ids=true, to_apply=%region_1.0 | all-reduce | flops 2 | bytes 16 | tf_op jit(solution)/shard_map/pmax | solution.py:139
  191.1 3.6 %collective-permute-start = (f32[5,4,3,128]{3,2,1,0:T(4,128)S(1)}, f32[5,4,3,128]{3,2,1,0:T(4,128)S(1)}, u32[]{:S(2)}, u32[]{:S(2)}) collective-permute-start(f32[5,4,3,128]{3,2,1,0:T(4,128)S(1)} %get-tuple-element.55), channel_id=1, source_target_pairs={{0,32},{32,64},{64,96},{96,128},{128,160},{160,192},{192,224},{224... | collective-permute-start | bytes 92168 | tf_op jit(solution)/shard_map/ppermute | solution.py:19
  194.8 2.9 collective-permute-start.17
  197.8 29.2 %all_gather.6 = f32[5,16,14,70]{3,2,0,1:T(8,128)S(1)} all-gather(f32[5,2,14,70]{3,2,0,1:T(8,128)S(1)} %pad_maximum_fusion.19), channel_id=1, replica_groups=mesh['gx'=16,'gy'=4,'gz'=8] {'gz'}, dimensions={1}, use_global_device_ids=true | all-gather | bytes 352800 | tf_op jit(solution)/shard_map/all_gather | solution.py:157
  233.0 9.2 %collective-permute-start.9 = (f32[3,4,24,4]{3,2,1,0:T(8,128)S(1)}, f32[3,4,24,4]{3,2,1,0:T(8,128)S(1)}, u32[]{:S(2)}, u32[]{:S(2)}) collective-permute-start(f32[3,4,24,4]{3,2,1,0:T(8,128)S(1)} %get-tuple-element.58), channel_id=1, source_target_pairs={{8,0},{16,8},{24,16},{0,24},{9,1},{17,9},{25,17},{1,25},{10,2},{18... | collective-permute-start | bytes 13832 | tf_op jit(solution)/shard_map/ppermute | solution.py:21
  247.3 4.6 %collective-permute-start.11 = (f32[3,4,24,136]{3,2,1,0:T(8,128)S(1)}, f32[3,4,24,136]{3,2,1,0:T(8,128)S(1)}, u32[]{:S(2)}, u32[]{:S(2)}) collective-permute-start(f32[3,4,24,136]{3,2,1,0:T(8,128)S(1)} %pad_maximum_fusion.10), channel_id=1, source_target_pairs={{1,0},{2,1},{3,2},{4,3},{5,4},{6,5},{7,6},{0,7},{9,8},{10,9},{11,1... | collective-permute-start | bytes 470024 | tf_op jit(solution)/shard_map/ppermute | solution.py:21
  254.5 3.2 collective-permute-start.2
  259.7 4.6 %collective-permute-done.3 = f32[5,4,22,3]{3,2,1,0:T(8,128)S(1)} collective-permute-done((f32[5,4,22,3]{3,2,1,0:T(8,128)S(1)}, f32[5,4,22,3]{3,2,1,0:T(8,128)S(1)}, u32[]{:S(2)}, u32[]{:S(2)}) %collective-permute-start.3) | collective-permute-done | bytes 5312 | tf_op jit(solution)/shard_map/ppermute | solution.py:21
  267.5 7.0 %collective-permute-start.5 = (f32[5,3,22,134]{3,2,1,0:T(8,128)S(1)}, f32[5,3,22,134]{3,2,1,0:T(8,128)S(1)}, u32[]{:S(2)}, u32[]{:S(2)}) collective-permute-start(f32[5,3,22,134]{3,2,1,0:T(8,128)S(1)} %get-tuple-element.42), channel_id=1, source_target_pairs={{1,0},{2,1},{3,2},{4,3},{5,4},{6,5},{7,6},{0,7},{9,8},{10,9},{11,1... | collective-permute-start | bytes 530648 | tf_op jit(solution)/shard_map/ppermute | solution.py:21
  277.3 3.2 collective-permute-start.18
  282.1 9.3 %collective-permute-done.19 = f32[3,16,16,4]{3,2,1,0:T(8,128)S(1)} collective-permute-done((f32[3,16,16,4]{3,2,1,0:T(8,128)S(1)}, f32[3,16,16,4]{3,2,1,0:T(8,128)S(1)}, u32[]{:S(2)}, u32[]{:S(2)}) %collective-permute-start.19) | collective-permute-done | bytes 12320 | tf_op jit(solution)/shard_map/ppermute | solution.py:21
  293.7 5.9 %fusion.27 = f32[3,16,8,72]{3,2,1,0:T(8,128)S(1)} fusion(f32[3,16,16,72]{3,2,1,0:T(8,128)S(1)} %pad_maximum_fusion.9, f32[]{:T(128)} %bitcast.14, f32[]{:T(128)} %bitcast.13, f32[]{:T(128)} %bitcast.12, f32[]{:T(128)} %bitcast.11, f32[]{:T(128)} %bitcast.10, f32[]{:T(128)} %bitcast.9, f32[]{:T(128)} %bitcast.8, f32[]{:T(128)} %bitcast.7, f32[]{:T(128)} %bitcast.6), kind=kLoop, calls=%fused_computation.85 | loop fusion | flops 470016 | bytes 1105956 | tf_op jit(solution)/shard_map/add | solution.py:123
  299.7 6.1 %fusion.19 = f32[3,16,8,64]{3,2,1,0:T(8,128)S(1)} fusion(f32[3,16,8,72]{3,2,1,0:T(8,128)S(1)} %fusion.27, f32[]{:T(128)} %bitcast.22, f32[]{:T(128)} %bitcast.21, f32[]{:T(128)} %bitcast.20, f32[]{:T(128)} %bitcast.19, f32[]{:T(128)} %bitcast.18, f32[]{:T(128)} %bitcast.17, f32[]{:T(128)} %bitcast.16, f32[]{:T(128)} %bitcast.15, f32[]{:T(128)} %bitcast.5), kind=kLoop, calls=%fused_computation.68 | loop fusion | flops 417792 | bytes 983076 | tf_op jit(solution)/shard_map/add | solution.py:123
  305.8 5.7 %fusion.66 = f32[3,2,8,64]{3,2,1,0:T(8,128)S(1)} fusion(f32[3,10,8,64]{3,2,1,0:T(8,128)S(1)} %fusion.44, f32[]{:T(128)} %bitcast.30, f32[]{:T(128)} %bitcast.29, f32[]{:T(128)} %bitcast.28, f32[]{:T(128)} %bitcast.27, f32[]{:T(128)} %bitcast.26, f32[]{:T(128)} %bitcast.25, f32[]{:T(128)} %bitcast.24, f32[]{:T(128)} %bitcast.23, f32[]{:T(128)} %bitcast.4), kind=kLoop, calls=%fused_computation.217 | loop fusion | flops 52224 | bytes 122916 | tf_op jit(solution)/shard_map/add | solution.py:123
  312.8 6.3 %fusion = f32[3,12,16,136]{3,2,1,0:T(8,128)S(1)} fusion(f32[3,12,24,136]{3,2,1,0:T(8,128)S(1)} %pad_maximum_fusion, f32[]{:T(128)} %bitcast.14, f32[]{:T(128)} %bitcast.13, f32[]{:T(128)} %bitcast.12, f32[]{:T(128)} %bitcast.11, f32[]{:T(128)} %bitcast.10, f32[]{:T(128)} %bitcast.9, f32[]{:T(128)} %bitcast.8, f32[]{:T(128)} %bitcast.7, f32[]{:T(128)} %bitcast.6), kind=kLoop, calls=%fused_computation.7 | loop fusion | flops 1331712 | bytes 3133476 | tf_op jit(solution)/shard_map/add | solution.py:123
  319.1 6.3 %fusion.11 = f32[3,12,16,128]{3,2,1,0:T(8,128)S(1)} fusion(f32[3,12,16,136]{3,2,1,0:T(8,128)S(1)} %fusion, f32[]{:T(128)} %bitcast.22, f32[]{:T(128)} %bitcast.21, f32[]{:T(128)} %bitcast.20, f32[]{:T(128)} %bitcast.19, f32[]{:T(128)} %bitcast.18, f32[]{:T(128)} %bitcast.17, f32[]{:T(128)} %bitcast.16, f32[]{:T(128)} %bitcast.15, f32[]{:T(128)} %bitcast.5), kind=kLoop, calls=%fused_computation.45 | loop fusion | flops 1253376 | bytes 2949156 | tf_op jit(solution)/shard_map/add | solution.py:123
  325.4 5.7 %fusion.45 = f32[3,4,16,128]{3,2,1,0:T(8,128)S(1)} fusion(f32[3,12,16,128]{3,2,1,0:T(8,128)S(1)} %fusion.11, f32[]{:T(128)} %bitcast.30, f32[]{:T(128)} %bitcast.29, f32[]{:T(128)} %bitcast.28, f32[]{:T(128)} %bitcast.27, f32[]{:T(128)} %bitcast.26, f32[]{:T(128)} %bitcast.25, f32[]{:T(128)} %bitcast.24, f32[]{:T(128)} %bitcast.23, f32[]{:T(128)} %bitcast.4), kind=kLoop, calls=%fused_computation.119 | loop fusion | flops 417792 | bytes 983076 | tf_op jit(solution)/shard_map/add | solution.py:123
  (129 shorter events, 46.2 us)
Async XLA Ops:
  1.5 231.4 %collective-permute-start.7 = (f32[3,4,4,128]{3,2,1,0:T(4,128)S(1)}, f32[3,4,4,128]{3,2,1,0:T(4,128)S(1)}, u32[]{:S(2)}, u32[]{:S(2)}) collective-permute-start(f32[3,4,4,128]{3,2,1,0:T(4,128)S(1)} %get-tuple-element.60), channel_id=1, source_target_pairs={{32,0},{64,32},{96,64},{128,96},{160,128},{192,160},{224,192},{256... | collective-permute-start | bytes 73736 | tf_op jit(solution)/shard_map/ppermute | solution.py:21
  13.4 219.4 %collective-permute-start.6 = (f32[3,4,4,128]{3,2,1,0:T(4,128)S(1)}, f32[3,4,4,128]{3,2,1,0:T(4,128)S(1)}, u32[]{:S(2)}, u32[]{:S(2)}) collective-permute-start(f32[3,4,4,128]{3,2,1,0:T(4,128)S(1)} %get-tuple-element.59), channel_id=1, source_target_pairs={{0,32},{32,64},{64,96},{96,128},{128,160},{160,192},{192,224},{224... | collective-permute-start | bytes 73736 | tf_op jit(solution)/shard_map/ppermute | solution.py:19
  16.3 235.6 %collective-permute-start.1 = (f32[5,4,3,128]{3,2,1,0:T(4,128)S(1)}, f32[5,4,3,128]{3,2,1,0:T(4,128)S(1)}, u32[]{:S(2)}, u32[]{:S(2)}) collective-permute-start(f32[5,4,3,128]{3,2,1,0:T(4,128)S(1)} %get-tuple-element.56), channel_id=1, source_target_pairs={{32,0},{64,32},{96,64},{128,96},{160,128},{192,160},{224,192},{256... | collective-permute-start | bytes 92168 | tf_op jit(solution)/shard_map/ppermute | solution.py:21
  21.8 52.9 %collective-permute-start.13 = (f32[5,2,3,64]{3,2,0,1:T(4,128)S(1)}, f32[5,2,3,64]{3,2,0,1:T(4,128)S(1)}, u32[]{:S(2)}, u32[]{:S(2)}) collective-permute-start(f32[5,2,3,64]{3,2,0,1:T(4,128)S(1)} %get-tuple-element.64), channel_id=1, source_target_pairs={{32,0},{64,32},{96,64},{128,96},{160,128},{192,160},{224,192},{256... | collective-permute-start | bytes 23048 | tf_op jit(solution)/shard_map/ppermute | solution.py:21
  23.7 51.0 %collective-permute-start.12 = (f32[5,2,3,64]{3,2,0,1:T(4,128)S(1)}, f32[5,2,3,64]{3,2,0,1:T(4,128)S(1)}, u32[]{:S(2)}, u32[]{:S(2)}) collective-permute-start(f32[5,2,3,64]{3,2,0,1:T(4,128)S(1)} %get-tuple-element.63), channel_id=1, source_target_pairs={{0,32},{32,64},{64,96},{96,128},{128,160},{160,192},{192,224},{224... | collective-permute-start | bytes 23048 | tf_op jit(solution)/shard_map/ppermute | solution.py:19
  33.7 8.4 %copy-start.5 = (s32[8]{0:T(128)S(1)}, s32[8]{0:T(128)}, u32[]{:S(2)}) copy-start(s32[8]{0:T(128)} %param.13) | copy-start | bytes 100
  42.8 31.9 %copy-start.2 = (f32[5,2,8,64]{3,2,1,0:T(8,128)S(1)}, f32[5,2,8,64]{3,2,1,0:T(8,128)}, u32[]{:S(2)}) copy-start(f32[5,2,8,64]{3,2,1,0:T(8,128)} %param.11) | copy-start | bytes 61444
  74.8 116.3 %collective-permute-start.15 = (f32[5,2,14,3]{3,2,0,1:T(8,128)S(1)}, f32[5,2,14,3]{3,2,0,1:T(8,128)S(1)}, u32[]{:S(2)}, u32[]{:S(2)}) collective-permute-start(f32[5,2,14,3]{3,2,0,1:T(8,128)S(1)} %get-tuple-element.62), channel_id=1, source_target_pairs={{8,0},{16,8},{24,16},{0,24},{9,1},{17,9},{25,17},{1,25},{10,2},{18... | collective-permute-start | bytes 5048 | tf_op jit(solution)/shard_map/ppermute | solution.py:21
  85.2 109.6 %collective-permute-start.14 = (f32[5,2,14,3]{3,2,0,1:T(8,128)S(1)}, f32[5,2,14,3]{3,2,0,1:T(8,128)S(1)}, u32[]{:S(2)}, u32[]{:S(2)}) collective-permute-start(f32[5,2,14,3]{3,2,0,1:T(8,128)S(1)} %get-tuple-element.61), channel_id=1, source_target_pairs={{0,8},{8,16},{16,24},{24,0},{1,9},{9,17},{17,25},{25,1},{2,10},{10... | collective-permute-start | bytes 5048 | tf_op jit(solution)/shard_map/ppermute | solution.py:19
  191.1 60.8 %collective-permute-start = (f32[5,4,3,128]{3,2,1,0:T(4,128)S(1)}, f32[5,4,3,128]{3,2,1,0:T(4,128)S(1)}, u32[]{:S(2)}, u32[]{:S(2)}) collective-permute-start(f32[5,4,3,128]{3,2,1,0:T(4,128)S(1)} %get-tuple-element.55), channel_id=1, source_target_pairs={{0,32},{32,64},{64,96},{96,128},{128,160},{160,192},{192,224},{224... | collective-permute-start | bytes 92168 | tf_op jit(solution)/shard_map/ppermute | solution.py:19
  194.8 79.7 %collective-permute-start.17 = (f32[3,16,4,64]{3,2,1,0:T(4,128)S(1)}, f32[3,16,4,64]{3,2,1,0:T(4,128)S(1)}, u32[]{:S(2)}, u32[]{:S(2)}) collective-permute-start(f32[3,16,4,64]{3,2,1,0:T(4,128)S(1)} %get-tuple-element.54), channel_id=1, source_target_pairs={{32,0},{64,32},{96,64},{128,96},{160,128},{192,160},{224,192},{256... | collective-permute-start | bytes 147464 | tf_op jit(solution)/shard_map/ppermute | solution.py:21
  231.4 20.5 %copy-start = (f32[5,4,16,128]{3,2,1,0:T(8,128)S(1)}, f32[5,4,16,128]{3,2,1,0:T(8,128)}, u32[]{:S(2)}) copy-start(f32[5,4,16,128]{3,2,1,0:T(8,128)} %param.8) | copy-start | bytes 491524
  233.0 11.6 %collective-permute-start.9 = (f32[3,4,24,4]{3,2,1,0:T(8,128)S(1)}, f32[3,4,24,4]{3,2,1,0:T(8,128)S(1)}, u32[]{:S(2)}, u32[]{:S(2)}) collective-permute-start(f32[3,4,24,4]{3,2,1,0:T(8,128)S(1)} %get-tuple-element.58), channel_id=1, source_target_pairs={{8,0},{16,8},{24,16},{0,24},{9,1},{17,9},{25,17},{1,25},{10,2},{18... | collective-permute-start | bytes 13832 | tf_op jit(solution)/shard_map/ppermute | solution.py:21
  242.2 4.8 %collective-permute-start.8 = (f32[3,4,24,4]{3,2,1,0:T(8,128)S(1)}, f32[3,4,24,4]{3,2,1,0:T(8,128)S(1)}, u32[]{:S(2)}, u32[]{:S(2)}) collective-permute-start(f32[3,4,24,4]{3,2,1,0:T(8,128)S(1)} %get-tuple-element.57), channel_id=1, source_target_pairs={{0,8},{8,16},{16,24},{24,0},{1,9},{9,17},{17,25},{25,1},{2,10},{10... | collective-permute-start | bytes 13832 | tf_op jit(solution)/shard_map/ppermute | solution.py:19
  244.6 29.9 %collective-permute-start.16 = (f32[3,16,4,64]{3,2,1,0:T(4,128)S(1)}, f32[3,16,4,64]{3,2,1,0:T(4,128)S(1)}, u32[]{:S(2)}, u32[]{:S(2)}) collective-permute-start(f32[3,16,4,64]{3,2,1,0:T(4,128)S(1)} %get-tuple-element.53), channel_id=1, source_target_pairs={{0,32},{32,64},{64,96},{96,128},{128,160},{160,192},{192,224},{224... | collective-permute-start | bytes 147464 | tf_op jit(solution)/shard_map/ppermute | solution.py:19
  247.3 65.3 %collective-permute-start.11 = (f32[3,4,24,136]{3,2,1,0:T(8,128)S(1)}, f32[3,4,24,136]{3,2,1,0:T(8,128)S(1)}, u32[]{:S(2)}, u32[]{:S(2)}) collective-permute-start(f32[3,4,24,136]{3,2,1,0:T(8,128)S(1)} %pad_maximum_fusion.10), channel_id=1, source_target_pairs={{1,0},{2,1},{3,2},{4,3},{5,4},{6,5},{7,6},{0,7},{9,8},{10,9},{11,1... | collective-permute-start | bytes 470024 | tf_op jit(solution)/shard_map/ppermute | solution.py:21
  252.1 12.2 %collective-permute-start.3 = (f32[5,4,22,3]{3,2,1,0:T(8,128)S(1)}, f32[5,4,22,3]{3,2,1,0:T(8,128)S(1)}, u32[]{:S(2)}, u32[]{:S(2)}) collective-permute-start(f32[5,4,22,3]{3,2,1,0:T(8,128)S(1)} %get-tuple-element.52), channel_id=1, source_target_pairs={{8,0},{16,8},{24,16},{0,24},{9,1},{17,9},{25,17},{1,25},{10,2},{18... | collective-permute-start | bytes 15848 | tf_op jit(solution)/shard_map/ppermute | solution.py:21
  254.5 11.7 %collective-permute-start.2 = (f32[5,4,22,3]{3,2,1,0:T(8,128)S(1)}, f32[5,4,22,3]{3,2,1,0:T(8,128)S(1)}, u32[]{:S(2)}, u32[]{:S(2)}) collective-permute-start(f32[5,4,22,3]{3,2,1,0:T(8,128)S(1)} %get-tuple-element.51), channel_id=1, source_target_pairs={{0,8},{8,16},{16,24},{24,0},{1,9},{9,17},{17,25},{25,1},{2,10},{10... | collective-permute-start | bytes 15848 | tf_op jit(solution)/shard_map/ppermute | solution.py:19
  264.3 48.3 %collective-permute-start.10 = (f32[3,4,24,136]{3,2,1,0:T(8,128)S(1)}, f32[3,4,24,136]{3,2,1,0:T(8,128)S(1)}, u32[]{:S(2)}, u32[]{:S(2)}) collective-permute-start(f32[3,4,24,136]{3,2,1,0:T(8,128)S(1)} %pad_maximum_fusion.10), channel_id=1, source_target_pairs={{0,1},{1,2},{2,3},{3,4},{4,5},{5,6},{6,7},{7,0},{8,9},{9,10},{10,1... | collective-permute-start | bytes 470024 | tf_op jit(solution)/shard_map/ppermute | solution.py:19
  267.5 63.7 %collective-permute-start.5 = (f32[5,3,22,134]{3,2,1,0:T(8,128)S(1)}, f32[5,3,22,134]{3,2,1,0:T(8,128)S(1)}, u32[]{:S(2)}, u32[]{:S(2)}) collective-permute-start(f32[5,3,22,134]{3,2,1,0:T(8,128)S(1)} %get-tuple-element.42), channel_id=1, source_target_pairs={{1,0},{2,1},{3,2},{4,3},{5,4},{6,5},{7,6},{0,7},{9,8},{10,9},{11,1... | collective-permute-start | bytes 530648 | tf_op jit(solution)/shard_map/ppermute | solution.py:21
  274.8 16.6 %collective-permute-start.19 = (f32[3,16,16,4]{3,2,1,0:T(8,128)S(1)}, f32[3,16,16,4]{3,2,1,0:T(8,128)S(1)}, u32[]{:S(2)}, u32[]{:S(2)}) collective-permute-start(f32[3,16,16,4]{3,2,1,0:T(8,128)S(1)} %get-tuple-element.48), channel_id=1, source_target_pairs={{8,0},{16,8},{24,16},{0,24},{9,1},{17,9},{25,17},{1,25},{10,2},{18... | collective-permute-start | bytes 36872 | tf_op jit(solution)/shard_map/ppermute | solution.py:21
  277.3 16.0 %collective-permute-start.18 = (f32[3,16,16,4]{3,2,1,0:T(8,128)S(1)}, f32[3,16,16,4]{3,2,1,0:T(8,128)S(1)}, u32[]{:S(2)}, u32[]{:S(2)}) collective-permute-start(f32[3,16,16,4]{3,2,1,0:T(8,128)S(1)} %get-tuple-element.47), channel_id=1, source_target_pairs={{0,8},{8,16},{16,24},{24,0},{1,9},{9,17},{17,25},{25,1},{2,10},{10... | collective-permute-start | bytes 36872 | tf_op jit(solution)/shard_map/ppermute | solution.py:19
  291.4 39.8 %collective-permute-start.4 = (f32[5,3,22,134]{3,2,1,0:T(8,128)S(1)}, f32[5,3,22,134]{3,2,1,0:T(8,128)S(1)}, u32[]{:S(2)}, u32[]{:S(2)}) collective-permute-start(f32[5,3,22,134]{3,2,1,0:T(8,128)S(1)} %get-tuple-element.41), channel_id=1, source_target_pairs={{0,1},{1,2},{2,3},{3,4},{4,5},{5,6},{6,7},{7,0},{8,9},{9,10},{10,1... | collective-permute-start | bytes 530648 | tf_op jit(solution)/shard_map/ppermute | solution.py:19
  293.7 18.1 %copy-start.4 = (f32[5,2,8,64]{3,2,1,0:T(8,128)S(1)}, f32[5,2,8,64]{3,2,1,0:T(8,128)}, u32[]{:S(2)}) copy-start(f32[5,2,8,64]{3,2,1,0:T(8,128)} %param.10) | copy-start | bytes 61444
  (2 other events, 4.7 us)
where the time goes:
time: 339 us; the launch traced here: 334 us
  blocking collectives  159 us (47%)
  starting transfers between devices  83.3 us (25%)
  other arithmetic  57 us (17%)
  local copies, waits for them, and re-layouts  17.4 us (5%)
  waiting for transfers between devices  14.1 us (4%)
  between operations  3.41 us (1%)
    pmax x1, blocking collectives, local(): lax.pmax((wave_speed_of(fine_section), wave_speed_of(coarse_section)), ('...  101 us
    ppermute x10, starting transfers between devices, padded_2(): lax.ppermute(head, axis, [((i + 1) % count, i) for i in range(count)])  57.3 us
    add x6, other arithmetic, conv_along(): total + taps[offset] * lax.slice_in_dim(extended, offset, offset + extent...  36 us
    all_gather x1, blocking collectives, local(): lax.all_gather(coarse_padded, 'gz', axis=1, tiled=True)  29.2 us
    all_gather x1, blocking collectives, local(): lax.all_gather(restricted, 'gz', axis=1, tiled=True)  28.5 us
    ppermute x10, starting transfers between devices, padded_2(): lax.ppermute(tail, axis, [(i, (i + 1) % count) for i in range(count)])  26 us
    ppermute x10, waiting for transfers between devices, padded_2(): lax.ppermute(head, axis, [((i + 1) % count, i) for i in range(count)])  14.1 us
    reshape x1, local copies, waits for them, and re-layouts, local(): fine_noise.reshape(3, half_z, 2, fine_noise.shape[2] // 2, 2, fine_noise....  8.43 us
  transfers between devices with their start and end apart: 20, of which 3 were waited for; matrix products, arithmetic and copies ran while one was open for 21% of the time, Pallas kernels for 0%

commit v1 on v0

v1 whole, which is shorter than its diff:
```python
import jax
import jax.numpy as jnp
from jax import lax
from jax.experimental import pallas as pl
from jax.experimental.pallas import tpu as pltpu
from jax.sharding import PartitionSpec as P

MESH = pl.DeviceIdType.MESH
GX, GY, GZ = 16, 4, 8
GAMMA = 1.4
SPEED_EPS = 3e-06
RESTRICT_SCALE = 0.35355339059327373
NEAR = [(i, j) for i in range(GY) for j in range(GZ) if (i, j) != (0, 0)]
ALONG = [8, 7, 9, 6, 10, 5, 11, 4, 12, 3, 13, 2, 14, 1, 15]
CLOSE = [1, 2, 3, 4, 12, 13, 14, 15]


def pressure_of(state, inverse):
    kinetic = 0.5 * (state[1] * state[1] + state[2] * state[2] + state[3] * state[3])
    return (GAMMA - 1.0) * (state[4] - kinetic * inverse)


def flux_entries(state, inverse, pressure, component):
    velocity = state[component] * inverse
    entries = [
        state[component],
        state[1] * velocity,
        state[2] * velocity,
        state[3] * velocity,
        (state[4] + pressure) * velocity,
    ]
    entries[component] = entries[component] + pressure
    return entries


def flux_alone(state, component):
    inverse = 1.0 / state[0]
    return flux_entries(state, inverse, pressure_of(state, inverse), component)


def fastest_of(state, inverse, pressure):
    largest = jnp.maximum(jnp.maximum(jnp.abs(state[1]), jnp.abs(state[2])), jnp.abs(state[3]))
    return largest * inverse + jnp.sqrt(GAMMA * pressure * inverse)


def side(low, mid, high, p, q, r, s):
    m0 = mid * high
    m1 = low * high
    m2 = low * mid
    w0 = m0 * m0
    w1 = 6.0 * (m1 * m1)
    w2 = 3.0 * (m2 * m2)
    total = w0 + w1 + w2
    sums = w0 * (5.0 * q - 2.0 * p) + w1 * (q + 2.0 * r) + w2 * (4.0 * r - s)
    guess = pl.reciprocal(total, approx=True)
    return sums * (guess * (2.0 - total * guess))


def indicators(steps):
    squares = [e * e for e in steps]
    low, mid, high = [], [], []
    for i in range(len(steps) - 1):
        cross = steps[i] * steps[i + 1]
        both = squares[i] + squares[i + 1] + SPEED_EPS
        base = both - 2.75 * cross
        low.append(base + 1.5 * squares[i + 1])
        high.append(base + 1.5 * squares[i])
        mid.append(both - 1.25 * cross)
    return low, mid, high


def sweep(flux_steps, state_steps, speed, cells):
    scaled = [speed * u for u in state_steps]
    up = [f + u for f, u in zip(flux_steps, scaled)]
    down = [f - u for f, u in zip(flux_steps, scaled)]
    low_u, mid_u, high_u = indicators(up)
    low_d, mid_d, high_d = indicators(down)
    faces = []
    for j in range(cells + 1):
        right = side(low_u[j], mid_u[j + 1], high_u[j + 2], up[j], up[j + 1], up[j + 2], up[j + 3])
        left = side(
            high_d[j + 3], mid_d[j + 2], low_d[j + 1], down[j + 4], down[j + 3], down[j + 2], down[j + 1]
        )
        faces.append(right - left)
    return [
        up[c + 2] + down[c + 3] + (faces[c + 1] - faces[c]) * (1.0 / 6.0) for c in range(cells)
    ]


def swap_halves(values):
    return pltpu.roll(values, 64, 1)


def kernel(
    us, noise, cs, taps, owner, fine_out, coarse_out,
    sp1, sp2, cp, fcp, ux, fx, ty, fy, uz, fz, nz, gat, nx, wx, nt, force, halves,
    dz, d16, d8, d1, az, a16, a8, a1,
    far_sem, s1_send, s1_recv, s2_send, s2_recv, gat_send, gat_recv, hs, hr,
):
    gx, gy, gz = lax.axis_index("gx"), lax.axis_index("gy"), lax.axis_index("gz")

    def near(step):
        return {"gy": lax.rem(gy + step[0], GY), "gz": lax.rem(gz + step[1], GZ)}

    def along(step):
        return {"gx": lax.rem(gx + step, GX)}

    barrier = pltpu.get_barrier_semaphore()
    for step in NEAR:
        pl.semaphore_signal(barrier, inc=1, device_id=near(step), device_id_type=MESH)
    for step in CLOSE:
        pl.semaphore_signal(barrier, inc=1, device_id=along(step), device_id_type=MESH)

    lane = lax.broadcasted_iota(jnp.int32, (8, 128), 1)
    first_half = lane < 64
    first_half_40 = lax.broadcasted_iota(jnp.int32, (40, 128), 1) < 64

    best = jnp.zeros((16, 128), jnp.float32)
    for z in range(4):
        state = [us[(f * 4 + z) * 16 : (f * 4 + z) * 16 + 16, :] for f in range(5)]
        inverse = 1.0 / state[0]
        pressure = pressure_of(state, inverse)
        best = jnp.maximum(best, fastest_of(state, inverse, pressure))
        for f, entry in enumerate(flux_entries(state, inverse, pressure, 2)):
            fy[(f * 4 + z) * 16 : (f * 4 + z) * 16 + 16, :] = entry
        for f, entry in enumerate(flux_entries(state, inverse, pressure, 3)):
            fz[f, 3 + z] = entry
        for f in range(5):
            uz[f, 3 + z] = state[f]
    best = jnp.maximum(best[0:8], best[8:16])
    for f in range(5):
        cp[f * 8 : f * 8 + 8, :] = jnp.concatenate(
            [cs[f * 16 : f * 16 + 8, :], cs[f * 16 + 8 : f * 16 + 16, :]], axis=1
        )
    coarse = [cp[f * 8 : f * 8 + 8, :] for f in range(5)]
    coarse_inverse = 1.0 / coarse[0]
    coarse_pressure = pressure_of(coarse, coarse_inverse)
    coarse_best = fastest_of(coarse, coarse_inverse, coarse_pressure)
    best = jnp.where(
        first_half,
        jnp.maximum(best, swap_halves(best)),
        jnp.maximum(coarse_best, swap_halves(coarse_best)),
    )
    sp1[31:32, :] = jnp.max(best, axis=0, keepdims=True)

    for c in range(3):
        for z in range(4):
            nz[c, 4 + z] = noise[(c * 4 + z) * 16 : (c * 4 + z) * 16 + 16, :]
        for pair in range(2):
            row = (c * 4 + 2 * pair) * 16
            halves[(c * 2 + pair) * 16 : (c * 2 + pair) * 16 + 16, :] = (
                noise[row : row + 16, :] + noise[row + 16 : row + 32, :]
            )
    from_lane = lax.broadcasted_iota(jnp.int32, (128, 128), 0)
    to_lane = lax.broadcasted_iota(jnp.int32, (128, 128), 1)
    restricted = jnp.zeros((24, 128), jnp.float32)
    for pair in range(2):
        rows = jnp.concatenate(
            [
                halves[pl.ds((c * 2 + pair) * 16, 8, stride=2), :]
                + halves[pl.ds((c * 2 + pair) * 16 + 1, 8, stride=2), :]
                for c in range(3)
            ],
            axis=0,
        )
        pick = (lax.shift_right_logical(from_lane, 1) + 64 * pair == to_lane).astype(jnp.float32)
        restricted = restricted + lax.dot(
            rows, pick, precision=lax.Precision.HIGHEST, preferred_element_type=jnp.float32
        )
    restricted = restricted * RESTRICT_SCALE
    for f in range(5):
        gat[gz, f] = coarse[f]
    for c in range(3):
        gat[gz, 5 + c] = restricted[c * 8 : c * 8 + 8]

    pl.semaphore_wait(barrier, len(NEAR) + len(CLOSE))
    for step in (4, GX - 4):
        pl.semaphore_signal(far_sem, inc=1, device_id=along(step), device_id_type=MESH)

    def send(index, src, dst, device):
        copy = pltpu.make_async_remote_copy(
            src_ref=src, dst_ref=dst, send_sem=hs.at[index], recv_sem=hr.at[index],
            device_id=device, device_id_type=MESH,
        )
        copy.start()
        return copy

    for n, step in enumerate(NEAR):
        pltpu.make_async_remote_copy(
            src_ref=sp1.at[pl.ds(31, 1)], dst_ref=sp1.at[pl.ds(n, 1)], send_sem=s1_send,
            recv_sem=s1_recv, device_id=near(step), device_id_type=MESH,
        ).start()
    next_z, last_z = near((0, 1)), near((0, GZ - 1))
    next_x, last_x = along(1), along(GX - 1)
    next_y, last_y = near((1, 0)), near((GY - 1, 0))
    noise_z = [
        send(0, nz.at[:, pl.ds(4, 4)], nz.at[:, pl.ds(0, 4)], next_z),
        send(1, nz.at[:, pl.ds(4, 4)], nz.at[:, pl.ds(8, 4)], last_z),
    ]
    for step in range(1, GZ):
        pltpu.make_async_remote_copy(
            src_ref=gat.at[gz], dst_ref=gat.at[gz], send_sem=gat_send, recv_sem=gat_recv.at[step - 1],
            device_id=near((0, step)), device_id_type=MESH,
        ).start()

    for k in range(16):
        for group in range(2):
            ux[(3 + k) * 32 + group * 8 : (3 + k) * 32 + group * 8 + 8, :] = us[
                pl.ds(group * 128 + k, 8, stride=16), :
            ]
        ux[(3 + k) * 32 + 16 : (3 + k) * 32 + 20, :] = us[pl.ds(256 + k, 4, stride=16), :]
    for k in range(8):
        row = cp[pl.ds(k, 5, stride=8), :]
        ux[(3 + k) * 32 + 24 : (3 + k) * 32 + 29, :] = row
        ux[(11 + k) * 32 + 24 : (11 + k) * 32 + 29, :] = row
    state_x = [
        send(2, ux.at[pl.ds(16 * 32, 96)], ux.at[pl.ds(0, 96)], next_x),
        send(3, ux.at[pl.ds(3 * 32, 96)], ux.at[pl.ds(19 * 32, 96)], last_x),
    ]

    for t in range(2):
        ty[t, 8:136, :] = us[t * 128 : t * 128 + 128, :].T
        ty[3 + t, 8:136, :] = fy[t * 128 : t * 128 + 128, :].T
    tail = us[256:320, :]
    ty[2, 8:136, :] = jnp.concatenate([tail, tail], axis=0).T
    tail = fy[256:320, :]
    ty[5, 8:136, :] = jnp.concatenate([tail, tail], axis=0).T
    for f, entry in enumerate(flux_entries(coarse, coarse_inverse, coarse_pressure, 2)):
        fcp[f * 8 : f * 8 + 8, :] = entry
    for t, ref in ((6, cp), (7, fcp)):
        packed = ref[0:40, :]
        swapped = swap_halves(packed)
        front = jnp.where(first_half_40, packed, swapped)
        back = jnp.where(first_half_40, swapped, packed)
        ty[t, 8:136, :] = jnp.concatenate([front, front[0:24], back, back[0:24]], axis=0).T
    state_y = [
        send(4, ty.at[:, pl.ds(128, 8)], ty.at[:, pl.ds(0, 8)], next_y),
        send(5, ty.at[:, pl.ds(8, 8)], ty.at[:, pl.ds(136, 8)], last_y),
    ]
    state_z = [
        send(6, uz.at[:, pl.ds(4, 3)], uz.at[:, pl.ds(0, 3)], next_z),
        send(7, uz.at[:, pl.ds(3, 3)], uz.at[:, pl.ds(7, 3)], last_z),
    ]

    def flux_x(k, carry):
        base = k * 32
        state = [ux[pl.ds(base + 4 * f, 4), :] for f in range(5)]
        for f, entry in enumerate(flux_alone(state, 1)):
            fx[pl.ds(base + 4 * f, 4), :] = entry
        return carry

    lax.fori_loop(3, 19, flux_x, 0)
    for f, entry in enumerate(flux_entries(coarse, coarse_inverse, coarse_pressure, 1)):
        fcp[f * 8 : f * 8 + 8, :] = entry
    for k in range(8):
        fx[(3 + k) * 32 + 24 : (3 + k) * 32 + 29, :] = fcp[pl.ds(k, 5, stride=8), :]

    def total_wait(ref, count, send_sem, recv_sem):
        return pltpu.make_async_remote_copy(
            src_ref=ref.at[pl.ds(0, count)], dst_ref=ref.at[pl.ds(0, count)], send_sem=send_sem,
            recv_sem=recv_sem, device_id=next_x, device_id_type=MESH,
        )

    first_round = total_wait(sp1, 31, s1_send, s1_recv)
    first_round.wait_recv()
    sp2[15:16, :] = jnp.max(sp1[...], axis=0, keepdims=True)
    pl.semaphore_wait(far_sem, 2)
    for n, step in enumerate(ALONG):
        pltpu.make_async_remote_copy(
            src_ref=sp2.at[pl.ds(15, 1)], dst_ref=sp2.at[pl.ds(n, 1)], send_sem=s2_send,
            recv_sem=s2_recv, device_id=along(step), device_id_type=MESH,
        ).start()

    for copy in noise_z:
        copy.wait_recv()

    def noise_along_z(c, carry):
        for h in range(2):
            planes = [nz[c, z, h * 8 : h * 8 + 8, :] for z in range(12)]
            for z in range(4):
                total = taps[2, 0] * planes[z]
                for t in range(1, 9):
                    total = total + taps[2, t] * planes[z + t]
                nx[c * 4 + z, 8 + h * 8 : 16 + h * 8, :] = total
        return carry

    lax.fori_loop(0, 3, noise_along_z, 0)
    for step in range(1, GZ):
        origin = lax.rem(gz + GZ - step, GZ)
        pltpu.make_async_remote_copy(
            src_ref=gat.at[gz], dst_ref=gat.at[origin], send_sem=gat_send, recv_sem=gat_recv.at[step - 1],
            device_id=next_x, device_id_type=MESH,
        ).wait_recv()
    block = jnp.int32(0)
    for j in range(GZ):
        block = block + j * (owner[j] == gz).astype(jnp.int32)

    def mixed(left, right):
        return jnp.where(first_half, swap_halves(left), swap_halves(right))

    around = [lax.rem(block + GZ + m, GZ) for m in range(-2, 3)]
    for c in range(3):
        pairs = [gat[j, 5 + c] for j in around]
        total = taps[2, 0] * pairs[0]
        for t in range(1, 9):
            plane = pairs[t // 2] if t % 2 == 0 else mixed(pairs[t // 2], pairs[t // 2 + 1])
            total = total + taps[2, t] * plane
        nx[12 + c, 8:16, :] = total
        nx[12 + c, 16:24, :] = total
    noise_x = [
        send(8, nx.at[:, pl.ds(16, 8)], nx.at[:, pl.ds(0, 8)], next_x),
        send(9, nx.at[:, pl.ds(8, 8)], nx.at[:, pl.ds(24, 8)], last_x),
    ]

    for copy in state_x:
        copy.wait_recv()
    lax.fori_loop(0, 3, flux_x, 0)
    lax.fori_loop(19, 22, flux_x, 0)
    for k in (0, 1, 2, 19, 20, 21):
        state = [ux[k * 32 + 24 + f : k * 32 + 25 + f, :] for f in range(5)]
        target = k if k < 3 else k - 8
        for f, entry in enumerate(flux_alone(state, 1)):
            fx[target * 32 + 24 + f : target * 32 + 25 + f, :] = entry
    state_x[1].wait_send()
    state_x[0].wait_send()
    for k in (11, 12, 13):
        ux[k * 32 + 24 : k * 32 + 32, :] = ux[(k + 8) * 32 + 24 : (k + 8) * 32 + 32, :]

    def steps_x(k, carry):
        for n, ref in enumerate((fx, ux)):
            for group in range(3):
                d16[n, group, k] = ref[pl.ds((k + 1) * 32 + group * 8, 8), :] - ref[
                    pl.ds(k * 32 + group * 8, 8), :
                ]
        return carry

    lax.fori_loop(0, 21, steps_x, 0)
    for n, ref in enumerate((fx, ux)):
        for k in range(13):
            d8[n, 0, k] = ref[(k + 1) * 32 + 24 : (k + 1) * 32 + 32, :] - ref[k * 32 + 24 : k * 32 + 32, :]

    for copy in noise_x:
        copy.wait_recv()

    def noise_along_x(n, carry):
        total = taps[0, 0] * nx[n, 4:20, :]
        for t in range(1, 9):
            total = total + taps[0, t] * nx[n, 4 + t : 20 + t, :]
        wx[pl.ds(pl.multiple_of(n * 16, 16), 16), :] = total
        return carry

    lax.fori_loop(0, 12, noise_along_x, 0)
    for c in range(3):
        total = taps[0, 0] * nx[12 + c, 4:12, :]
        for t in range(1, 9):
            base = 4 + t if t <= 4 else 12 + t
            total = total + taps[0, t] * nx[12 + c, base : base + 8, :]
        swapped = swap_halves(total)
        wx[192 + c * 8 : 200 + c * 8, :] = jnp.where(first_half, total, swapped)
        wx[216 + c * 8 : 224 + c * 8, :] = jnp.where(first_half, swapped, total)
    for t in range(2):
        nt[t, 8:136, :] = wx[t * 128 : t * 128 + 128, :].T
    noise_y = [
        send(10, nt.at[:, pl.ds(128, 8)], nt.at[:, pl.ds(0, 8)], next_y),
        send(11, nt.at[:, pl.ds(8, 8)], nt.at[:, pl.ds(136, 8)], last_y),
    ]

    for copy in state_y:
        copy.wait_recv()
    for n in range(2):

        def steps_y(t, carry):
            rows = [ty[3 - 3 * n + t, pl.ds(5 + k, 8, stride=16), :] for k in range(22)]
            for k in range(21):
                d16[n, 3 + t, k] = rows[k + 1] - rows[k]
            return carry

        lax.fori_loop(0, 3, steps_y, 0)
    for copy in state_y:
        copy.wait_send()
    for n, t in enumerate((7, 6)):
        ty[t, 72:80, :] = ty[t, 136:144, :]
        rows = [ty[t, pl.ds(5 + k, 8, stride=8), :] for k in range(14)]
        for k in range(13):
            d8[n, 1, k] = rows[k + 1] - rows[k]

    for copy in state_z:
        copy.wait_recv()
    for k in (0, 1, 2, 7, 8, 9):
        state = [uz[f, k] for f in range(5)]
        for f, entry in enumerate(flux_alone(state, 3)):
            fz[f, k] = entry

    def steps_z(f, carry):
        for n, ref in enumerate((fz, uz)):
            for h in range(2):
                for k in range(9):
                    d4 = ref[f, k + 1, h * 8 : h * 8 + 8, :] - ref[f, k, h * 8 : h * 8 + 8, :]
                    dz[n, f * 2 + h, k] = d4
        return carry

    lax.fori_loop(0, 5, steps_z, 0)
    pairs_u, pairs_f = [], []
    for j in around:
        state = [gat[owner[j], f] for f in range(5)]
        pairs_u.append(state)
        pairs_f.append(flux_alone(state, 3))
    for n, pairs in enumerate((pairs_f, pairs_u)):
        for f in range(5):
            planes = []
            for j in range(-3, 4):
                m = (j + 4) // 2
                planes.append(pairs[m][f] if j % 2 == 0 else mixed(pairs[m][f], pairs[m + 1][f]))
            for k in range(6):
                d1[n, f, k] = planes[k + 1] - planes[k]

    for copy in noise_y:
        copy.wait_recv()
    total = taps[1, 0] * nt[0, 4:132, :]
    for t in range(1, 9):
        total = total + taps[1, t] * nt[0, 4 + t : 132 + t, :]
    force[0:128, :] = total.T
    left = taps[1, 0] * nt[1, 4:132, :]
    for t in range(1, 5):
        left = left + taps[1, t] * nt[1, 4 + t : 132 + t, :]
    total = left
    for t in range(5, 9):
        total = total + taps[1, t] * nt[1, 4 + t : 132 + t, :]
    own = left[0:64]
    for t in range(5, 9):
        own = own + taps[1, t] * nt[1, 68 + t : 132 + t, :]
    front = jnp.where(lax.broadcasted_iota(jnp.int32, (64, 128), 1) < 64, total[0:64], own)
    force[128:256, :] = jnp.concatenate([front, total[64:128]], axis=0).T

    second_round = total_wait(sp2, 15, s2_send, s2_recv)
    second_round.wait_recv()
    speeds = jnp.max(sp2[...], axis=0, keepdims=True)
    front_row = lax.broadcasted_iota(jnp.int32, (1, 128), 1) < 64
    speed_fine = jnp.broadcast_to(
        jnp.max(jnp.where(front_row, speeds, 0.0), axis=1, keepdims=True), (8, 128)
    )
    speed_coarse = jnp.broadcast_to(
        jnp.max(jnp.where(front_row, 0.0, speeds), axis=1, keepdims=True), (8, 128)
    )

    def sweep_16(g, carry):
        out = sweep([d16[0, g, k] for k in range(21)], [d16[1, g, k] for k in range(21)], speed_fine, 16)
        for k in range(16):
            a16[pl.ds(g * 128 + k, 8, stride=16), :] = out[k]
        return carry

    def sweep_4(g, carry):
        out = sweep([dz[0, g, k] for k in range(9)], [dz[1, g, k] for k in range(9)], speed_fine, 4)
        for z in range(4):
            az[g, z] = out[z]
        return carry

    def sweep_8(g, carry):
        out = sweep([d8[0, g, k] for k in range(13)], [d8[1, g, k] for k in range(13)], speed_coarse, 8)
        for k in range(8):
            a8[pl.ds(g * 64 + k, 8, stride=8), :] = out[k]
        return carry

    def sweep_1(g, carry):
        out = sweep([d1[0, g, k] for k in range(6)], [d1[1, g, k] for k in range(6)], speed_coarse, 1)
        a1[g] = out[0]
        return carry

    lax.fori_loop(0, 6, sweep_16, 0)
    lax.fori_loop(0, 10, sweep_4, 0)
    lax.fori_loop(0, 2, sweep_8, 0)
    lax.fori_loop(0, 5, sweep_1, 0)

    for t in range(3):
        wide = a16[384 + t * 128 : 512 + t * 128, :].T
        a16[384 + t * 128 : 512 + t * 128, :] = wide
    rate_fine = 0.1 / speed_fine
    rate_coarse = 0.1 / speed_coarse
    for z in range(4):
        for h in range(2):
            state, push = [], []
            for f in range(5):
                row = (f * 4 + z) * 16 + h * 8
                state.append(us[row : row + 8, :])
            for c in range(3):
                row = (c * 4 + z) * 16 + h * 8
                push.append(force[row : row + 8, :])
            work = state[1] * push[0] + state[2] * push[1] + state[3] * push[2]
            source = [None, state[0] * push[0], state[0] * push[1], state[0] * push[2], work]
            for f in range(5):
                row = (f * 4 + z) * 16 + h * 8
                change = -0.5 * (a16[row : row + 8, :] + a16[384 + row : 392 + row, :] + az[f * 2 + h, z])
                if source[f] is not None:
                    change = change + source[f]
                fine_out[row : row + 8, :] = 0.25 * state[f] + rate_fine * change

    along_y = a8[64:128, :]
    turned = jnp.concatenate([along_y, along_y], axis=0).T
    along_y = jnp.where(first_half_40, turned[0:40], turned[64:104])
    push = []
    for c in range(3):
        push.append(
            jnp.where(
                first_half,
                force[192 + c * 8 : 200 + c * 8, :],
                swap_halves(force[216 + c * 8 : 224 + c * 8, :]),
            )
        )
    state = [cp[f * 8 : f * 8 + 8, :] for f in range(5)]
    work = state[1] * push[0] + state[2] * push[1] + state[3] * push[2]
    source = [None, state[0] * push[0], state[0] * push[1], state[0] * push[2], work]
    for f in range(5):
        change = -0.5 * (a8[f * 8 : f * 8 + 8, :] + along_y[f * 8 : f * 8 + 8] + a1[f])
        if source[f] is not None:
            change = change + 2.0 * source[f]
        result = 0.25 * state[f] + rate_coarse * change
        coarse_out[f * 16 : f * 16 + 8, :] = result[:, 0:64]
        coarse_out[f * 16 + 8 : f * 16 + 16, :] = swap_halves(result)[:, 0:64]

    first_round.wait_send()
    second_round.wait_send()
    for copy in noise_z + state_z + noise_x + noise_y:
        copy.wait_send()
    pltpu.make_async_remote_copy(
        src_ref=gat.at[pl.ds(0, 7)], dst_ref=gat.at[pl.ds(0, 7)], send_sem=gat_send,
        recv_sem=gat_recv.at[0], device_id=next_x, device_id_type=MESH,
    ).wait_send()


def local(fine_start, fine_section, fine_noise, coarse_start, coarse_section, taps, owner):
    f32 = jnp.float32
    vmem = pl.BlockSpec(memory_space=pltpu.VMEM)
    smem = pl.BlockSpec(memory_space=pltpu.SMEM)
    dma = pltpu.SemaphoreType.DMA
    fine, coarse = pl.pallas_call(
        kernel,
        out_shape=(jax.ShapeDtypeStruct((320, 128), f32), jax.ShapeDtypeStruct((80, 64), f32)),
        in_specs=[vmem, vmem, vmem, smem, smem],
        out_specs=(vmem, vmem),
        scratch_shapes=[
            pltpu.VMEM((32, 128), f32),
            pltpu.VMEM((16, 128), f32),
            pltpu.VMEM((40, 128), f32),
            pltpu.VMEM((40, 128), f32),
            pltpu.VMEM((704, 128), f32),
            pltpu.VMEM((704, 128), f32),
            pltpu.VMEM((8, 144, 128), f32),
            pltpu.VMEM((320, 128), f32),
            pltpu.VMEM((5, 10, 16, 128), f32),
            pltpu.VMEM((5, 10, 16, 128), f32),
            pltpu.VMEM((3, 12, 16, 128), f32),
            pltpu.VMEM((8, 8, 8, 128), f32),
            pltpu.VMEM((15, 32, 128), f32),
            pltpu.VMEM((256, 128), f32),
            pltpu.VMEM((2, 144, 128), f32),
            pltpu.VMEM((256, 128), f32),
            pltpu.VMEM((96, 128), f32),
            pltpu.VMEM((2, 10, 9, 8, 128), f32),
            pltpu.VMEM((2, 6, 21, 8, 128), f32),
            pltpu.VMEM((2, 2, 13, 8, 128), f32),
            pltpu.VMEM((2, 5, 6, 8, 128), f32),
            pltpu.VMEM((10, 4, 8, 128), f32),
            pltpu.VMEM((768, 128), f32),
            pltpu.VMEM((128, 128), f32),
            pltpu.VMEM((5, 8, 128), f32),
            pltpu.SemaphoreType.REGULAR,
            dma, dma, dma, dma, dma, dma((7,)), dma((12,)), dma((12,)),
        ],
        compiler_params=pltpu.CompilerParams(
            collective_id=0, has_side_effects=True, vmem_limit_bytes=24 * 1024 * 1024
        ),
        name="section",
    )(
        fine_section.reshape(320, 128), fine_noise.reshape(192, 128), coarse_section.reshape(80, 64),
        taps, owner,
    )
    return (
        0.75 * fine_start + fine.reshape(fine_start.shape),
        0.75 * coarse_start + coarse.reshape(coarse_start.shape),
    )


def solution(mesh):
    cells = P(None, "gz", "gx", "gy")
    return jax.shard_map(
        local,
        mesh=mesh,
        in_specs=(cells, cells, cells, cells, cells, P(), P()),
        out_specs=(cells, cells),
        check_vma=False,
    )
```

time: 339 us -> 40 us (0.12); the launches traced: 334 us -> 39.7 us
  blocking collectives: 159 us -> 0 us
  starting transfers between devices: 83.3 us -> 0 us
  other arithmetic: 57 us -> 1.32 us
  Pallas kernels: 0 us -> 34.4 us
  waiting for transfers between devices: 14.1 us -> 0 us
  local copies, waits for them, and re-layouts: 17.4 us -> 3.34 us
    pmax x1 -> x0, blocking collectives: 101 us -> none  [local(): lax.pmax((wave_speed_of(fine_section), wave_speed_of(coarse_section)), ('...]
    ppermute x20 -> x0, starting transfers between devices: 83.3 us -> none  [the longest x10 57.3 us: padded_2(): lax.ppermute(head, axis, [((i + 1) % count, i) for i in range(count)])]
    all_gather x2 -> x0, blocking collectives: 57.7 us -> none  [the longest x1 29.2 us: local(): lax.all_gather(coarse_padded, 'gz', axis=1, tiled=True)]
    add x14 -> x2, other arithmetic: 42.3 us -> 1.32 us  [the longest x1 0.7 us: local(): 0.75 * fine_start + fine.reshape(fine_start.shape)]
    pallas_call x0 -> x1, Pallas kernels: none -> 34.4 us  [local(): pl.pallas_call(kernel, out_shape=(jax.ShapeDtypeStruct((320, 128), f32),...]
    ppermute x20 -> x0, waiting for transfers between devices: 14.1 us -> none  [the longest x10 14.1 us: padded_2(): lax.ppermute(head, axis, [((i + 1) % count, i) for i in range(count)])]
    reshape x2 -> x0, local copies, waits for them, and re-layouts: 8.72 us -> none  [the longest x1 8.43 us: local(): fine_noise.reshape(3, half_z, 2, fine_noise.shape[2] // 2, 2, fine_noise....]
    slice x11 -> x0, local copies, waits for them, and re-layouts: 6.95 us -> none  [the longest x9 3.21 us: padded_2(): lax.slice_in_dim(cells, cells.shape[dim] - width, cells.shape[dim], axis=...]
  transfers between devices with their start and end apart: 20 -> 0, of which waited for: 3 -> 0; matrix products, arithmetic and copies ran while one was open for 21% -> 0% of each run, Pallas kernels for 0% -> 0%
where the time goes in v1:
time: 40 us; the launch traced here: 39.7 us
  Pallas kernels  34.4 us (86%)
  local copies, waits for them, and re-layouts  3.34 us (8%)
  other arithmetic  1.32 us (3%)
  between operations  0.68 us (2%)
    pallas_call x1, Pallas kernels, local(): pl.pallas_call(kernel, out_shape=(jax.ShapeDtypeStruct((320, 128), f32),...  34.4 us
    unnamed x14, local copies, waits for them, and re-layouts  3.34 us

profile of v1, /device:TPU:1, one launch (start us, length us, event | category | flops | bytes accessed | tf_op | source)
XLA Modules:
  0.0 39.7 jit_solution(1630720399033386853)
XLA Ops:
  0.6 0.0 copy-start.3
  0.6 0.0 copy-start.4
  0.7 0.7 %copy-done.3 = f32[3,9]{1,0:T(4,128)S(1)} copy-done((f32[3,9]{1,0:T(4,128)S(1)}, f32[3,9]{1,0:T(4,128)}, u32[]{:S(2)}) %copy-start.3) | copy-done | bytes 132
  1.3 0.0 copy-done.4
  1.3 0.0 copy-start
  1.3 0.9 %copy-done = f32[5,4,16,128]{3,2,1,0:T(8,128)S(1)} copy-done((f32[5,4,16,128]{3,2,1,0:T(8,128)S(1)}, f32[5,4,16,128]{3,2,1,0:T(8,128)}, u32[]{:S(2)}) %copy-start) | copy-done | bytes 163864
  2.2 0.0 copy-start.1
  2.2 0.9 %copy-done.1 = f32[3,4,16,128]{3,2,1,0:T(8,128)S(1)} copy-done((f32[3,4,16,128]{3,2,1,0:T(8,128)S(1)}, f32[3,4,16,128]{3,2,1,0:T(8,128)}, u32[]{:S(2)}) %copy-start.1) | copy-done | bytes 98328
  3.1 0.0 copy-start.2
  3.1 0.8 %copy-done.2 = f32[5,2,8,64]{3,2,1,0:T(8,128)S(1)} copy-done((f32[5,2,8,64]{3,2,1,0:T(8,128)S(1)}, f32[5,2,8,64]{3,2,1,0:T(8,128)}, u32[]{:S(2)}) %copy-start.2) | copy-done | bytes 20504
  3.9 0.0 copy-start.5
  3.9 34.4 %section.1 = (f32[320,128]{1,0:T(8,128)S(1)}, f32[80,64]{1,0:T(8,128)S(1)}) custom-call(f32[320,128]{1,0:T(8,128)S(1)} %bitcast.5, f32[192,128]{1,0:T(8,128)S(1)} %bitcast.7, f32[80,64]{1,0:T(8,128)S(1)} %bitcast.8, f32[3,9]{1,0:T(4,128)S(1)} %copy-done.3, s32[8]{0:T(128)S(1)} %copy-done.4), custom_call_target="tpu_custom_call" | custom-call | tf_op jit(solution)/shard_map/section/pallas_call | solution.py:535
  38.3 0.0 copy-done.5
  38.3 0.0 copy-start.6
  38.3 0.7 %multiply_add_fusion = f32[5,4,16,128]{3,2,1,0:T(8,128)} fusion(f32[5,4,16,128]{3,2,1,0:T(8,128)S(1)} %bitcast.6, f32[5,4,16,128]{3,2,1,0:T(8,128)S(1)} %copy-done.5), kind=kLoop, calls=%fused_computation | loop fusion | flops 81920 | bytes 491520 | tf_op jit(solution)/shard_map/add | solution.py:578
  39.0 0.1 copy-done.6
  39.1 0.6 %multiply_add_fusion.1 = f32[5,2,8,64]{3,2,1,0:T(8,128)} fusion(f32[5,2,8,64]{3,2,1,0:T(8,128)S(1)} %bitcast.9, f32[5,2,8,64]{3,2,1,0:T(8,128)S(1)} %copy-done.6), kind=kLoop, calls=%fused_computation.1 | loop fusion | flops 10240 | bytes 61440 | tf_op jit(solution)/shard_map/add | solution.py:579
Async XLA Ops:
  0.6 0.7 %copy-start.3 = (f32[3,9]{1,0:T(4,128)S(1)}, f32[3,9]{1,0:T(4,128)}, u32[]{:S(2)}) copy-start(f32[3,9]{1,0:T(4,128)} %taps.1) | copy-start | bytes 328
  0.6 0.7 %copy-start.4 = (s32[8]{0:T(128)S(1)}, s32[8]{0:T(128)}, u32[]{:S(2)}) copy-start(s32[8]{0:T(128)} %owner.1) | copy-start | bytes 100
  1.3 0.9 %copy-start = (f32[5,4,16,128]{3,2,1,0:T(8,128)S(1)}, f32[5,4,16,128]{3,2,1,0:T(8,128)}, u32[]{:S(2)}) copy-start(f32[5,4,16,128]{3,2,1,0:T(8,128)} %param.8) | copy-start | bytes 491524
  2.2 0.9 %copy-start.1 = (f32[3,4,16,128]{3,2,1,0:T(8,128)S(1)}, f32[3,4,16,128]{3,2,1,0:T(8,128)}, u32[]{:S(2)}) copy-start(f32[3,4,16,128]{3,2,1,0:T(8,128)} %param.9) | copy-start | bytes 294916
  3.1 0.8 %copy-start.2 = (f32[5,2,8,64]{3,2,1,0:T(8,128)S(1)}, f32[5,2,8,64]{3,2,1,0:T(8,128)}, u32[]{:S(2)}) copy-start(f32[5,2,8,64]{3,2,1,0:T(8,128)} %param.11) | copy-start | bytes 61444
  3.9 34.4 %copy-start.5 = (f32[5,4,16,128]{3,2,1,0:T(8,128)S(1)}, f32[5,4,16,128]{3,2,1,0:T(8,128)}, u32[]{:S(2)}) copy-start(f32[5,4,16,128]{3,2,1,0:T(8,128)} %param.7) | copy-start | bytes 491524
  38.3 0.8 %copy-start.6 = (f32[5,2,8,64]{3,2,1,0:T(8,128)S(1)}, f32[5,2,8,64]{3,2,1,0:T(8,128)}, u32[]{:S(2)}) copy-start(f32[5,2,8,64]{3,2,1,0:T(8,128)} %param.10) | copy-start | bytes 61444

commit v2 on v1

--- a/solution.py
+++ b/solution.py
@@ -13,6 +13,7 @@
 NEAR = [(i, j) for i in range(GY) for j in range(GZ) if (i, j) != (0, 0)]
 ALONG = [8, 7, 9, 6, 10, 5, 11, 4, 12, 3, 13, 2, 14, 1, 15]
 CLOSE = [1, 2, 3, 4, 12, 13, 14, 15]
+CORNERS = [(1, 1), (1, GY - 1), (GX - 1, 1), (GX - 1, GY - 1)]
 
 
 def pressure_of(state, inverse):
@@ -92,11 +93,19 @@
 
 
 def kernel(
-    us, noise, cs, taps, owner, fine_out, coarse_out,
-    sp1, sp2, cp, fcp, ux, fx, ty, fy, uz, fz, nz, gat, nx, wx, nt, force, halves,
-    dz, d16, d8, d1, az, a16, a8, a1,
-    far_sem, s1_send, s1_recv, s2_send, s2_recv, gat_send, gat_recv, hs, hr,
+    us_hbm, noise_hbm, cs_hbm, taps_hbm, owner_hbm, fine_out, coarse_out,
+    us, noise, cs, taps, owner, sp1, sp2, cp, fcp, ux, fx, ty, fy, uz, fz, nz, gs, gr, nx, pk, hb, wx, nt,
+    force, halves, dz, d16, d8, d1, az, a16, a8, a1,
+    ins, far_sem, s1_send, s1_recv, s2_send, s2_recv, gs_send, gs_recv, gr_send, gr_recv, hs, hr,
 ):
+    loads = [
+        pltpu.make_async_copy(src, dst, ins.at[n])
+        for n, (src, dst) in enumerate(
+            ((us_hbm, us), (cs_hbm, cs), (noise_hbm, noise), (taps_hbm, taps), (owner_hbm, owner))
+        )
+    ]
+    for load in loads:
+        load.start()
     gx, gy, gz = lax.axis_index("gx"), lax.axis_index("gy"), lax.axis_index("gz")
 
     def near(step):
@@ -105,16 +114,19 @@
     def along(step):
         return {"gx": lax.rem(gx + step, GX)}
 
+    def corner(step):
+        return {"gx": lax.rem(gx + step[0], GX), "gy": lax.rem(gy + step[1], GY)}
+
     barrier = pltpu.get_barrier_semaphore()
-    for step in NEAR:
-        pl.semaphore_signal(barrier, inc=1, device_id=near(step), device_id_type=MESH)
-    for step in CLOSE:
-        pl.semaphore_signal(barrier, inc=1, device_id=along(step), device_id_type=MESH)
+    greeted = [near(step) for step in NEAR] + [along(step) for step in CLOSE] + [corner(step) for step in CORNERS]
+    for device in greeted:
+        pl.semaphore_signal(barrier, inc=1, device_id=device, device_id_type=MESH)
 
     lane = lax.broadcasted_iota(jnp.int32, (8, 128), 1)
     first_half = lane < 64
     first_half_40 = lax.broadcasted_iota(jnp.int32, (40, 128), 1) < 64
 
+    loads[0].wait()
     best = jnp.zeros((16, 128), jnp.float32)
     for z in range(4):
         state = [us[(f * 4 + z) * 16 : (f * 4 + z) * 16 + 16, :] for f in range(5)]
@@ -128,6 +140,7 @@
         for f in range(5):
             uz[f, 3 + z] = state[f]
     best = jnp.maximum(best[0:8], best[8:16])
+    loads[1].wait()
     for f in range(5):
         cp[f * 8 : f * 8 + 8, :] = jnp.concatenate(
             [cs[f * 16 : f * 16 + 8, :], cs[f * 16 + 8 : f * 16 + 16, :]], axis=1
@@ -143,14 +156,25 @@
     )
     sp1[31:32, :] = jnp.max(best, axis=0, keepdims=True)
 
+    for load in loads[2:]:
+        load.wait()
+    eighth = jnp.bitwise_and(lane, 7)
+    group_of_lane = lax.shift_right_logical(lane, 3)
+    packed = [jnp.zeros((8, 128), jnp.float32) for _ in range(2)]
     for c in range(3):
         for z in range(4):
-            nz[c, 4 + z] = noise[(c * 4 + z) * 16 : (c * 4 + z) * 16 + 16, :]
+            n = c * 4 + z
+            for h in range(2):
+                tile = noise[n * 16 + h * 8 : n * 16 + h * 8 + 8, :]
+                nx[n, 8 + h * 8 : 16 + h * 8, :] = tile
+                packed[h] = jnp.where(group_of_lane == n, pltpu.roll(tile, (n * 8 + 4) % 128, 1), packed[h])
         for pair in range(2):
             row = (c * 4 + 2 * pair) * 16
             halves[(c * 2 + pair) * 16 : (c * 2 + pair) * 16 + 16, :] = (
                 noise[row : row + 16, :] + noise[row + 16 : row + 32, :]
             )
+    for h in range(2):
+        pk[0, h * 8 : h * 8 + 8, :] = packed[h]
     from_lane = lax.broadcasted_iota(jnp.int32, (128, 128), 0)
     to_lane = lax.broadcasted_iota(jnp.int32, (128, 128), 1)
     restricted = jnp.zeros((24, 128), jnp.float32)
@@ -168,40 +192,20 @@
             rows, pick, precision=lax.Precision.HIGHEST, preferred_element_type=jnp.float32
         )
     restricted = restricted * RESTRICT_SCALE
+    coarse_packed = jnp.zeros((8, 128), jnp.float32)
+    for c in range(3):
+        tile = restricted[c * 8 : c * 8 + 8]
+        nx[12 + c, 8:16, :] = tile
+        nx[12 + c, 16:24, :] = tile
+        swapped = swap_halves(tile)
+        for p in range(2):
+            m = c * 2 + p
+            doubled = jnp.where(first_half, tile, swapped) if p == 0 else jnp.where(first_half, swapped, tile)
+            coarse_packed = jnp.where(group_of_lane == m, pltpu.roll(doubled, m * 8 + 4, 1), coarse_packed)
+    pk[1, 0:8, :] = coarse_packed
+    pk[1, 8:16, :] = coarse_packed
     for f in range(5):
-        gat[gz, f] = coarse[f]
-    for c in range(3):
-        gat[gz, 5 + c] = restricted[c * 8 : c * 8 + 8]
-
-    pl.semaphore_wait(barrier, len(NEAR) + len(CLOSE))
-    for step in (4, GX - 4):
-        pl.semaphore_signal(far_sem, inc=1, device_id=along(step), device_id_type=MESH)
-
-    def send(index, src, dst, device):
-        copy = pltpu.make_async_remote_copy(
-            src_ref=src, dst_ref=dst, send_sem=hs.at[index], recv_sem=hr.at[index],
-            device_id=device, device_id_type=MESH,
-        )
-        copy.start()
-        return copy
-
-    for n, step in enumerate(NEAR):
-        pltpu.make_async_remote_copy(
-            src_ref=sp1.at[pl.ds(31, 1)], dst_ref=sp1.at[pl.ds(n, 1)], send_sem=s1_send,
-            recv_sem=s1_recv, device_id=near(step), device_id_type=MESH,
-        ).start()
-    next_z, last_z = near((0, 1)), near((0, GZ - 1))
-    next_x, last_x = along(1), along(GX - 1)
-    next_y, last_y = near((1, 0)), near((GY - 1, 0))
-    noise_z = [
-        send(0, nz.at[:, pl.ds(4, 4)], nz.at[:, pl.ds(0, 4)], next_z),
-        send(1, nz.at[:, pl.ds(4, 4)], nz.at[:, pl.ds(8, 4)], last_z),
-    ]
-    for step in range(1, GZ):
-        pltpu.make_async_remote_copy(
-            src_ref=gat.at[gz], dst_ref=gat.at[gz], send_sem=gat_send, recv_sem=gat_recv.at[step - 1],
-            device_id=near((0, step)), device_id_type=MESH,
-        ).start()
+        gs[gz, f] = coarse[f]
 
     for k in range(16):
         for group in range(2):
@@ -213,10 +217,6 @@
         row = cp[pl.ds(k, 5, stride=8), :]
         ux[(3 + k) * 32 + 24 : (3 + k) * 32 + 29, :] = row
         ux[(11 + k) * 32 + 24 : (11 + k) * 32 + 29, :] = row
-    state_x = [
-        send(2, ux.at[pl.ds(16 * 32, 96)], ux.at[pl.ds(0, 96)], next_x),
-        send(3, ux.at[pl.ds(3 * 32, 96)], ux.at[pl.ds(19 * 32, 96)], last_x),
-    ]
 
     for t in range(2):
         ty[t, 8:136, :] = us[t * 128 : t * 128 + 128, :].T
@@ -228,19 +228,77 @@
     for f, entry in enumerate(flux_entries(coarse, coarse_inverse, coarse_pressure, 2)):
         fcp[f * 8 : f * 8 + 8, :] = entry
     for t, ref in ((6, cp), (7, fcp)):
-        packed = ref[0:40, :]
-        swapped = swap_halves(packed)
-        front = jnp.where(first_half_40, packed, swapped)
-        back = jnp.where(first_half_40, swapped, packed)
+        both = ref[0:40, :]
+        swapped = swap_halves(both)
+        front = jnp.where(first_half_40, both, swapped)
+        back = jnp.where(first_half_40, swapped, both)
         ty[t, 8:136, :] = jnp.concatenate([front, front[0:24], back, back[0:24]], axis=0).T
+
+    pl.semaphore_wait(barrier, len(greeted))
+    next_z, last_z = near((0, 1)), near((0, GZ - 1))
+    next_x, last_x = along(1), along(GX - 1)
+    next_y, last_y = near((1, 0)), near((GY - 1, 0))
+
+    def send(index, src, dst, device):
+        copy = pltpu.make_async_remote_copy(
+            src_ref=src, dst_ref=dst, send_sem=hs.at[index], recv_sem=hr.at[index],
+            device_id=device, device_id_type=MESH,
+        )
+        copy.start()
+        return copy
+
+    for n, step in enumerate(NEAR):
+        pltpu.make_async_remote_copy(
+            src_ref=sp1.at[pl.ds(31, 1)], dst_ref=sp1.at[pl.ds(n, 1)], send_sem=s1_send,
+            recv_sem=s1_recv, device_id=near(step), device_id_type=MESH,
+        ).start()
+    for step in (4, GX - 4):
+        pl.semaphore_signal(far_sem, inc=1, device_id=along(step), device_id_type=MESH)
+    noise_xy = [
+        send(0, nx.at[:, pl.ds(16, 8)], nx.at[:, pl.ds(0, 8)], next_x),
+        send(1, nx.at[:, pl.ds(8, 8)], nx.at[:, pl.ds(24, 8)], last_x),
+        send(2, pk, hb.at[0, :, pl.ds(8, 16)], next_y),
+        send(3, pk, hb.at[1, :, pl.ds(8, 16)], last_y),
+        send(4, pk.at[:, pl.ds(8, 8)], hb.at[0, :, pl.ds(0, 8)], corner(CORNERS[0])),
+        send(5, pk.at[:, pl.ds(8, 8)], hb.at[1, :, pl.ds(0, 8)], corner(CORNERS[1])),
+        send(6, pk.at[:, pl.ds(0, 8)], hb.at[0, :, pl.ds(24, 8)], corner(CORNERS[2])),
+        send(7, pk.at[:, pl.ds(0, 8)], hb.at[1, :, pl.ds(24, 8)], corner(CORNERS[3])),
+    ]
+    state_x = [
+        send(8, ux.at[pl.ds(16 * 32, 96)], ux.at[pl.ds(0, 96)], next_x),
+        send(9, ux.at[pl.ds(3 * 32, 96)], ux.at[pl.ds(19 * 32, 96)], last_x),
+    ]
     state_y = [
-        send(4, ty.at[:, pl.ds(128, 8)], ty.at[:, pl.ds(0, 8)], next_y),
-        send(5, ty.at[:, pl.ds(8, 8)], ty.at[:, pl.ds(136, 8)], last_y),
+        send(10, ty.at[:, pl.ds(128, 8)], ty.at[:, pl.ds(0, 8)], next_y),
+        send(11, ty.at[:, pl.ds(8, 8)], ty.at[:, pl.ds(136, 8)], last_y),
     ]
     state_z = [
-        send(6, uz.at[:, pl.ds(4, 3)], uz.at[:, pl.ds(0, 3)], next_z),
-        send(7, uz.at[:, pl.ds(3, 3)], uz.at[:, pl.ds(7, 3)], last_z),
-    ]
+        send(12, uz.at[:, pl.ds(4, 3)], uz.at[:, pl.ds(0, 3)], next_z),
+        send(13, uz.at[:, pl.ds(3, 3)], uz.at[:, pl.ds(7, 3)], last_z),
+    ]
+
+    def column(ref, send_sem, recv_sem):
+        copies = []
+        for step in range(1, GZ):
+            copy = pltpu.make_async_remote_copy(
+                src_ref=ref.at[gz], dst_ref=ref.at[gz], send_sem=send_sem, recv_sem=recv_sem.at[step - 1],
+                device_id=near((0, step)), device_id_type=MESH,
+            )
+            copy.start()
+            origin = lax.rem(gz + GZ - step, GZ)
+            copies.append(
+                pltpu.make_async_remote_copy(
+                    src_ref=ref.at[gz], dst_ref=ref.at[origin], send_sem=send_sem,
+                    recv_sem=recv_sem.at[step - 1], device_id=next_z, device_id_type=MESH,
+                )
+            )
+        whole = pltpu.make_async_remote_copy(
+            src_ref=ref.at[pl.ds(0, GZ - 1)], dst_ref=ref.at[pl.ds(0, GZ - 1)], send_sem=send_sem,
+            recv_sem=recv_sem.at[0], device_id=next_z, device_id_type=MESH,
+        )
+        return copies, whole
+
+    state_column, state_column_sent = column(gs, gs_send, gs_recv)
 
     def flux_x(k, carry):
         base = k * 32
@@ -271,46 +329,83 @@
             recv_sem=s2_recv, device_id=along(step), device_id_type=MESH,
         ).start()
 
-    for copy in noise_z:
+    for copy in noise_xy:
         copy.wait_recv()
 
-    def noise_along_z(c, carry):
-        for h in range(2):
-            planes = [nz[c, z, h * 8 : h * 8 + 8, :] for z in range(12)]
-            for z in range(4):
-                total = taps[2, 0] * planes[z]
-                for t in range(1, 9):
-                    total = total + taps[2, t] * planes[z + t]
-                nx[c * 4 + z, 8 + h * 8 : 16 + h * 8, :] = total
-        return carry
-
-    lax.fori_loop(0, 3, noise_along_z, 0)
-    for step in range(1, GZ):
-        origin = lax.rem(gz + GZ - step, GZ)
-        pltpu.make_async_remote_copy(
-            src_ref=gat.at[gz], dst_ref=gat.at[origin], send_sem=gat_send, recv_sem=gat_recv.at[step - 1],
-            device_id=next_x, device_id_type=MESH,
-        ).wait_recv()
-    block = jnp.int32(0)
-    for j in range(GZ):
-        block = block + j * (owner[j] == gz).astype(jnp.int32)
-
-    def mixed(left, right):
-        return jnp.where(first_half, swap_halves(left), swap_halves(right))
-
-    around = [lax.rem(block + GZ + m, GZ) for m in range(-2, 3)]
+    def noise_along_x(n, carry):
+        total = taps[0, 0] * nx[n, 4:20, :]
+        for t in range(1, 9):
+            total = total + taps[0, t] * nx[n, 4 + t : 20 + t, :]
+        wx[pl.ds(pl.multiple_of(n * 16, 16), 16), :] = total
+        return carry
+
+    lax.fori_loop(0, 12, noise_along_x, 0)
     for c in range(3):
-        pairs = [gat[j, 5 + c] for j in around]
-        total = taps[2, 0] * pairs[0]
+        total = taps[0, 0] * nx[12 + c, 4:12, :]
         for t in range(1, 9):
-            plane = pairs[t // 2] if t % 2 == 0 else mixed(pairs[t // 2], pairs[t // 2 + 1])
-            total = total + taps[2, t] * plane
-        nx[12 + c, 8:16, :] = total
-        nx[12 + c, 16:24, :] = total
-    noise_x = [
-        send(8, nx.at[:, pl.ds(16, 8)], nx.at[:, pl.ds(0, 8)], next_x),
-        send(9, nx.at[:, pl.ds(8, 8)], nx.at[:, pl.ds(24, 8)], last_x),
-    ]
+            base = 4 + t if t <= 4 else 12 + t
+            total = total + taps[0, t] * nx[12 + c, base : base + 8, :]
+        swapped = swap_halves(total)
+        wx[192 + c * 8 : 200 + c * 8, :] = jnp.where(first_half, total, swapped)
+        wx[216 + c * 8 : 224 + c * 8, :] = jnp.where(first_half, swapped, total)
+    for b in range(2):
+        for r in range(4):
+            hb[0, b, r * 8 : r * 8 + 8, :] = jnp.where(
+                eighth < 4, hb[0, b, r * 8 : r * 8 + 8, :], hb[1, b, r * 8 : r * 8 + 8, :]
+            )
+    beside = taps[0, 0] * hb[0, 0, 4:20, :]
+    for t in range(1, 9):
+        beside = beside + taps[0, t] * hb[0, 0, 4 + t : 20 + t, :]
+    coarse_beside = taps[0, 0] * hb[0, 1, 4:12, :]
+    for t in range(1, 9):
+        base = 4 + t if t <= 4 else 12 + t
+        coarse_beside = coarse_beside + taps[0, t] * hb[0, 1, base : base + 8, :]
+
+    turned = jnp.concatenate([beside, coarse_beside, jnp.zeros((104, 128), jnp.float32)], axis=0).T
+    rims = [jnp.zeros((8, 128), jnp.float32) for _ in range(2)]
+    sixteenth = lax.shift_right_logical(lane, 4)
+    for n in range(12):
+        shift = (n % 8) * 16
+        rolled = pltpu.roll(turned[n * 8 : n * 8 + 8], shift, 1) if shift else turned[n * 8 : n * 8 + 8]
+        rims[n // 8] = jnp.where(sixteenth == n % 8, rolled, rims[n // 8])
+    for c in range(3):
+        for p in range(2):
+            m = c * 2 + p
+            target = 64 + p * 24 + c * 8
+            rolled = pltpu.roll(turned[m * 8 : m * 8 + 8], target - 16, 1)
+            rims[1] = jnp.where(group_of_lane == target // 8, rolled, rims[1])
+    for t in range(2):
+        nt[t, 8:136, :] = wx[t * 128 : t * 128 + 128, :].T
+        nt[t, 4:8, :] = rims[t][0:4]
+        nt[t, 136:140, :] = rims[t][4:8]
+    total = taps[1, 0] * nt[0, 4:132, :]
+    for t in range(1, 9):
+        total = total + taps[1, t] * nt[0, 4 + t : 132 + t, :]
+    total = total.T
+    for n in range(8):
+        nz[n // 4, 4 + n % 4] = total[n * 16 : n * 16 + 16]
+    left = taps[1, 0] * nt[1, 4:132, :]
+    for t in range(1, 5):
+        left = left + taps[1, t] * nt[1, 4 + t : 132 + t, :]
+    total = left
+    for t in range(5, 9):
+        total = total + taps[1, t] * nt[1, 4 + t : 132 + t, :]
+    own = left[0:64]
+    for t in range(5, 9):
+        own = own + taps[1, t] * nt[1, 68 + t : 132 + t, :]
+    front = jnp.where(lax.broadcasted_iota(jnp.int32, (64, 128), 1) < 64, total[0:64], own)
+    total = jnp.concatenate([front, total[64:128]], axis=0).T
+    for n in range(8, 12):
+        nz[n // 4, 4 + n % 4] = total[(n - 8) * 16 : (n - 8) * 16 + 16]
+    for c in range(3):
+        gr[gz, c] = jnp.where(
+            first_half, total[64 + c * 8 : 72 + c * 8], swap_halves(total[88 + c * 8 : 96 + c * 8])
+        )
+    noise_z = [
+        send(14, nz.at[:, pl.ds(4, 4)], nz.at[:, pl.ds(0, 4)], next_z),
+        send(15, nz.at[:, pl.ds(4, 4)], nz.at[:, pl.ds(8, 4)], last_z),
+    ]
+    noise_column, noise_column_sent = column(gr, gr_send, gr_recv)
 
     for copy in state_x:
         copy.wait_recv()
@@ -321,8 +416,8 @@
         target = k if k < 3 else k - 8
         for f, entry in enumerate(flux_alone(state, 1)):
             fx[target * 32 + 24 + f : target * 32 + 25 + f, :] = entry
-    state_x[1].wait_send()
-    state_x[0].wait_send()
+    for copy in state_x:
+        copy.wait_send()
     for k in (11, 12, 13):
         ux[k * 32 + 24 : k * 32 + 32, :] = ux[(k + 8) * 32 + 24 : (k + 8) * 32 + 32, :]
 
@@ -338,32 +433,6 @@
     for n, ref in enumerate((fx, ux)):
         for k in range(13):
             d8[n, 0, k] = ref[(k + 1) * 32 + 24 : (k + 1) * 32 + 32, :] - ref[k * 32 + 24 : k * 32 + 32, :]
-
-    for copy in noise_x:
-        copy.wait_recv()
-
-    def noise_along_x(n, carry):
-        total = taps[0, 0] * nx[n, 4:20, :]
-        for t in range(1, 9):
-            total = total + taps[0, t] * nx[n, 4 + t : 20 + t, :]
-        wx[pl.ds(pl.multiple_of(n * 16, 16), 16), :] = total
-        return carry
-
-    lax.fori_loop(0, 12, noise_along_x, 0)
-    for c in range(3):
-        total = taps[0, 0] * nx[12 + c, 4:12, :]
-        for t in range(1, 9):
-            base = 4 + t if t <= 4 else 12 + t
-            total = total + taps[0, t] * nx[12 + c, base : base + 8, :]
-        swapped = swap_halves(total)
-        wx[192 + c * 8 : 200 + c * 8, :] = jnp.where(first_half, total, swapped)
-        wx[216 + c * 8 : 224 + c * 8, :] = jnp.where(first_half, swapped, total)
-    for t in range(2):
-        nt[t, 8:136, :] = wx[t * 128 : t * 128 + 128, :].T
-    noise_y = [
-        send(10, nt.at[:, pl.ds(128, 8)], nt.at[:, pl.ds(0, 8)], next_y),
-        send(11, nt.at[:, pl.ds(8, 8)], nt.at[:, pl.ds(136, 8)], last_y),
-    ]
 
     for copy in state_y:
         copy.wait_recv()
@@ -400,9 +469,19 @@
         return carry
 
     lax.fori_loop(0, 5, steps_z, 0)
+    block = jnp.int32(0)
+    for j in range(GZ):
+        block = block + j * (owner[j] == gz).astype(jnp.int32)
+
+    def mixed(left, right):
+        return jnp.where(first_half, swap_halves(left), swap_halves(right))
+
+    around = [lax.rem(block + GZ + m, GZ) for m in range(-2, 3)]
+    for copy in state_column:
+        copy.wait_recv()
     pairs_u, pairs_f = [], []
     for j in around:
-        state = [gat[owner[j], f] for f in range(5)]
+        state = [gs[owner[j], f] for f in range(5)]
         pairs_u.append(state)
         pairs_f.append(flux_alone(state, 3))
     for n, pairs in enumerate((pairs_f, pairs_u)):
@@ -414,23 +493,44 @@
             for k in range(6):
                 d1[n, f, k] = planes[k + 1] - planes[k]
 
-    for copy in noise_y:
+    for copy in noise_z:
         copy.wait_recv()
-    total = taps[1, 0] * nt[0, 4:132, :]
-    for t in range(1, 9):
-        total = total + taps[1, t] * nt[0, 4 + t : 132 + t, :]
-    force[0:128, :] = total.T
-    left = taps[1, 0] * nt[1, 4:132, :]
-    for t in range(1, 5):
-        left = left + taps[1, t] * nt[1, 4 + t : 132 + t, :]
-    total = left
-    for t in range(5, 9):
-        total = total + taps[1, t] * nt[1, 4 + t : 132 + t, :]
-    own = left[0:64]
-    for t in range(5, 9):
-        own = own + taps[1, t] * nt[1, 68 + t : 132 + t, :]
-    front = jnp.where(lax.broadcasted_iota(jnp.int32, (64, 128), 1) < 64, total[0:64], own)
-    force[128:256, :] = jnp.concatenate([front, total[64:128]], axis=0).T
+    for h in range(2):
+
+        def noise_along_z(c, carry):
+            planes = [nz[c, z, h * 8 : h * 8 + 8, :] for z in range(12)]
+            for z in range(4):
+                total = taps[2, 0] * planes[z]
+                for t in range(1, 9):
+                    total = total + taps[2, t] * planes[z + t]
+                force[c * 4 + z, h * 8 : h * 8 + 8, :] = total
+            return carry
+
+        lax.fori_loop(0, 3, noise_along_z, 0)
+
+    def sources(z, carry):
+        state = [us[pl.ds(pl.multiple_of((f * 4 + z) * 16, 16), 16), :] for f in range(4)]
+        push = [force[c * 4 + z] for c in range(3)]
+        for c in range(3):
+            force[c * 4 + z] = state[0] * push[c]
+        force[12 + z] = state[1] * push[0] + state[2] * push[1] + state[3] * push[2]
+        return carry
+
+    lax.fori_loop(0, 4, sources, 0)
+    for copy in noise_column:
+        copy.wait_recv()
+    push = []
+    for c in range(3):
+        pairs = [gr[j, c] for j in around]
+        total = taps[2, 0] * pairs[0]
+        for t in range(1, 9):
+            plane = pairs[t // 2] if t % 2 == 0 else mixed(pairs[t // 2], pairs[t // 2 + 1])
+            total = total + taps[2, t] * plane
+        push.append(2.0 * total)
+    work = coarse[1] * push[0] + coarse[2] * push[1] + coarse[3] * push[2]
+    coarse_source = [None, coarse[0] * push[0], coarse[0] * push[1], coarse[0] * push[2], work]
+    for f in range(1, 5):
+        fcp[f * 8 : f * 8 + 8, :] = coarse_source[f]
 
     second_round = total_wait(sp2, 15, s2_send, s2_recv)
     second_round.wait_recv()
@@ -471,73 +571,54 @@
     lax.fori_loop(0, 2, sweep_8, 0)
     lax.fori_loop(0, 5, sweep_1, 0)
 
+    rate_fine = 0.1 / speed_fine
+    rate_coarse = 0.1 / speed_coarse
     for t in range(3):
         wide = a16[384 + t * 128 : 512 + t * 128, :].T
-        a16[384 + t * 128 : 512 + t * 128, :] = wide
-    rate_fine = 0.1 / speed_fine
-    rate_coarse = 0.1 / speed_coarse
-    for z in range(4):
-        for h in range(2):
-            state, push = [], []
-            for f in range(5):
-                row = (f * 4 + z) * 16 + h * 8
-                state.append(us[row : row + 8, :])
-            for c in range(3):
-                row = (c * 4 + z) * 16 + h * 8
-                push.append(force[row : row + 8, :])
-            work = state[1] * push[0] + state[2] * push[1] + state[3] * push[2]
-            source = [None, state[0] * push[0], state[0] * push[1], state[0] * push[2], work]
-            for f in range(5):
-                row = (f * 4 + z) * 16 + h * 8
-                change = -0.5 * (a16[row : row + 8, :] + a16[384 + row : 392 + row, :] + az[f * 2 + h, z])
-                if source[f] is not None:
-                    change = change + source[f]
-                fine_out[row : row + 8, :] = 0.25 * state[f] + rate_fine * change
+        for tile in range(16 if t < 2 else 8):
+            index = t * 16 + tile
+            f, z, h = index // 8, (index // 2) % 4, index % 2
+            row = index * 8
+            change = -0.5 * (a16[row : row + 8, :] + wide[tile * 8 : tile * 8 + 8] + az[f * 2 + h, z])
+            if f > 0:
+                change = change + force[(f - 1) * 4 + z, h * 8 : h * 8 + 8, :]
+            fine_out[row : row + 8, :] = 0.25 * us[row : row + 8, :] + rate_fine * change
 
     along_y = a8[64:128, :]
     turned = jnp.concatenate([along_y, along_y], axis=0).T
     along_y = jnp.where(first_half_40, turned[0:40], turned[64:104])
-    push = []
-    for c in range(3):
-        push.append(
-            jnp.where(
-                first_half,
-                force[192 + c * 8 : 200 + c * 8, :],
-                swap_halves(force[216 + c * 8 : 224 + c * 8, :]),
-            )
-        )
-    state = [cp[f * 8 : f * 8 + 8, :] for f in range(5)]
-    work = state[1] * push[0] + state[2] * push[1] + state[3] * push[2]
-    source = [None, state[0] * push[0], state[0] * push[1], state[0] * push[2], work]
     for f in range(5):
         change = -0.5 * (a8[f * 8 : f * 8 + 8, :] + along_y[f * 8 : f * 8 + 8] + a1[f])
-        if source[f] is not None:
-            change = change + 2.0 * source[f]
-        result = 0.25 * state[f] + rate_coarse * change
+        if f > 0:
+            change = change + fcp[f * 8 : f * 8 + 8, :]
+        result = 0.25 * cp[f * 8 : f * 8 + 8, :] + rate_coarse * change
         coarse_out[f * 16 : f * 16 + 8, :] = result[:, 0:64]
         coarse_out[f * 16 + 8 : f * 16 + 16, :] = swap_halves(result)[:, 0:64]
 
     first_round.wait_send()
     second_round.wait_send()
-    for copy in noise_z + state_z + noise_x + noise_y:
+    for copy in noise_xy + state_z + noise_z:
         copy.wait_send()
-    pltpu.make_async_remote_copy(
-        src_ref=gat.at[pl.ds(0, 7)], dst_ref=gat.at[pl.ds(0, 7)], send_sem=gat_send,
-        recv_sem=gat_recv.at[0], device_id=next_x, device_id_type=MESH,
-    ).wait_send()
+    state_column_sent.wait_send()
+    noise_column_sent.wait_send()
 
 
 def local(fine_start, fine_section, fine_noise, coarse_start, coarse_section, taps, owner):
     f32 = jnp.float32
     vmem = pl.BlockSpec(memory_space=pltpu.VMEM)
-    smem = pl.BlockSpec(memory_space=pltpu.SMEM)
+    hbm = pl.BlockSpec(memory_space=pltpu.HBM)
     dma = pltpu.SemaphoreType.DMA
     fine, coarse = pl.pallas_call(
         kernel,
         out_shape=(jax.ShapeDtypeStruct((320, 128), f32), jax.ShapeDtypeStruct((80, 64), f32)),
-        in_specs=[vmem, vmem, vmem, smem, smem],
+        in_specs=[hbm] * 5,
         out_specs=(vmem, vmem),
         scratch_shapes=[
+            pltpu.VMEM((320, 128), f32),
+            pltpu.VMEM((192, 128), f32),
+            pltpu.VMEM((80, 64), f32),
+            pltpu.SMEM((3, 9), f32),
+            pltpu.SMEM((8,), jnp.int32),
             pltpu.VMEM((32, 128), f32),
             pltpu.VMEM((16, 128), f32),
             pltpu.VMEM((40, 128), f32),
@@ -549,11 +630,14 @@
             pltpu.VMEM((5, 10, 16, 128), f32),
             pltpu.VMEM((5, 10, 16, 128), f32),
             pltpu.VMEM((3, 12, 16, 128), f32),
-            pltpu.VMEM((8, 8, 8, 128), f32),
+            pltpu.VMEM((8, 5, 8, 128), f32),
+            pltpu.VMEM((8, 3, 8, 128), f32),
             pltpu.VMEM((15, 32, 128), f32),
+            pltpu.VMEM((2, 16, 128), f32),
+            pltpu.VMEM((2, 2, 32, 128), f32),
             pltpu.VMEM((256, 128), f32),
             pltpu.VMEM((2, 144, 128), f32),
-            pltpu.VMEM((256, 128), f32),
+            pltpu.VMEM((16, 16, 128), f32),
             pltpu.VMEM((96, 128), f32),
             pltpu.VMEM((2, 10, 9, 8, 128), f32),
             pltpu.VMEM((2, 6, 21, 8, 128), f32),
@@ -563,16 +647,22 @@
             pltpu.VMEM((768, 128), f32),
             pltpu.VMEM((128, 128), f32),
             pltpu.VMEM((5, 8, 128), f32),
+            dma((5,)),
             pltpu.SemaphoreType.REGULAR,
-            dma, dma, dma, dma, dma, dma((7,)), dma((12,)), dma((12,)),
+            dma, dma, dma, dma, dma, dma((7,)), dma, dma((7,)), dma((16,)), dma((16,)),
         ],
         compiler_params=pltpu.CompilerParams(
             collective_id=0, has_side_effects=True, vmem_limit_bytes=24 * 1024 * 1024
         ),
         name="section",
     )(
-        fine_section.reshape(320, 128), fine_noise.reshape(192, 128), coarse_section.reshape(80, 64),
-        taps, owner,
+        *(
+            pltpu.with_memory_space_constraint(operand, pltpu.HBM)
+            for operand in (
+                fine_section.reshape(320, 128), fine_noise.reshape(192, 128),
+                coarse_section.reshape(80, 64), taps, owner,
+            )
+        )
     )
     return (
         0.75 * fine_start + fine.reshape(fine_start.shape),

time: 40 us -> 33.7 us (0.84)
  local copies, waits for them, and re-layouts: 3.34 us -> 0.08 us
  Pallas kernels: 34.4 us -> 31.4 us
    unnamed x14 -> x4, local copies, waits for them, and re-layouts: 3.34 us -> 0.08 us
    pallas_call x1, Pallas kernels: 34.4 us -> 31.4 us  [local(): pl.pallas_call(kernel, out_shape=(jax.ShapeDtypeStruct((320, 128), f32),...]
where the time goes in v2:
time: 33.7 us; the launch traced here: 33.5 us
  Pallas kernels  31.4 us (93%)
  other arithmetic  1.32 us (4%)
  between operations  0.66 us (2%)
    pallas_call x1, Pallas kernels, local(): pl.pallas_call(kernel, out_shape=(jax.ShapeDtypeStruct((320, 128), f32),...  31.4 us
    add x1, other arithmetic, local(): 0.75 * fine_start + fine.reshape(fine_start.shape)  0.7 us

profile of v2, /device:TPU:1, one launch (start us, length us, event | category | flops | bytes accessed | tf_op | source)
XLA Modules:
  0.0 33.5 jit_solution(10541811826631145993)
XLA Ops:
  0.6 0.0 copy-start
  0.6 31.4 %section.1 = (f32[320,128]{1,0:T(8,128)S(1)}, f32[80,64]{1,0:T(8,128)S(1)}) custom-call(f32[320,128]{1,0:T(8,128)} %bitcast.7, f32[192,128]{1,0:T(8,128)} %bitcast.8, f32[80,64]{1,0:T(8,128)} %bitcast.9, f32[3,9]{1,0:T(4,128)} %taps_hbm.1, s32[8]{0:T(128)} %owner_hbm.1), custom_call_target="tpu_custom_call" | custom-call | tf_op jit(solution)/shard_map/section/pallas_call | solution.py:611
  32.1 0.0 copy-done
  32.1 0.0 copy-start.1
  32.1 0.7 %multiply_add_fusion = f32[5,4,16,128]{3,2,1,0:T(8,128)} fusion(f32[5,4,16,128]{3,2,1,0:T(8,128)S(1)} %bitcast.5, f32[5,4,16,128]{3,2,1,0:T(8,128)S(1)} %copy-done), kind=kLoop, calls=%fused_computation | loop fusion | flops 81920 | bytes 491520 | tf_op jit(solution)/shard_map/add | solution.py:668
  32.8 0.1 copy-done.1
  32.9 0.6 %multiply_add_fusion.1 = f32[5,2,8,64]{3,2,1,0:T(8,128)} fusion(f32[5,2,8,64]{3,2,1,0:T(8,128)S(1)} %bitcast.6, f32[5,2,8,64]{3,2,1,0:T(8,128)S(1)} %copy-done.1), kind=kLoop, calls=%fused_computation.1 | loop fusion | flops 10240 | bytes 61440 | tf_op jit(solution)/shard_map/add | solution.py:669
Async XLA Ops:
  0.6 31.4 %copy-start = (f32[5,4,16,128]{3,2,1,0:T(8,128)S(1)}, f32[5,4,16,128]{3,2,1,0:T(8,128)}, u32[]{:S(2)}) copy-start(f32[5,4,16,128]{3,2,1,0:T(8,128)} %param.7) | copy-start | bytes 491524
  32.1 0.8 %copy-start.1 = (f32[5,2,8,64]{3,2,1,0:T(8,128)S(1)}, f32[5,2,8,64]{3,2,1,0:T(8,128)}, u32[]{:S(2)}) copy-start(f32[5,2,8,64]{3,2,1,0:T(8,128)} %param.10) | copy-start | bytes 61444

commit v3 on v2

--- a/solution.py
+++ b/solution.py
@@ -10,9 +10,12 @@
 GAMMA = 1.4
 SPEED_EPS = 3e-06
 RESTRICT_SCALE = 0.35355339059327373
-NEAR = [(i, j) for i in range(GY) for j in range(GZ) if (i, j) != (0, 0)]
+NEAR = sorted(
+    ((i, j) for i in range(GY) for j in range(GZ) if (i, j) != (0, 0)),
+    key=lambda step: -((step[0] + 1) // 2 % 2 + 2 * (step[1] // 4) + min(step[1] % 4, -step[1] % 4)),
+)
 ALONG = [8, 7, 9, 6, 10, 5, 11, 4, 12, 3, 13, 2, 14, 1, 15]
-CLOSE = [1, 2, 3, 4, 12, 13, 14, 15]
+CLOSE = [4, 12, 3, 13, 2, 14, 1, 15]
 CORNERS = [(1, 1), (1, GY - 1), (GX - 1, 1), (GX - 1, GY - 1)]
 
 
@@ -118,7 +121,7 @@
         return {"gx": lax.rem(gx + step[0], GX), "gy": lax.rem(gy + step[1], GY)}
 
     barrier = pltpu.get_barrier_semaphore()
-    greeted = [near(step) for step in NEAR] + [along(step) for step in CLOSE] + [corner(step) for step in CORNERS]
+    greeted = [along(step) for step in CLOSE] + [near(step) for step in NEAR] + [corner(step) for step in CORNERS]
     for device in greeted:
         pl.semaphore_signal(barrier, inc=1, device_id=device, device_id_type=MESH)
 
@@ -207,33 +210,6 @@
     for f in range(5):
         gs[gz, f] = coarse[f]
 
-    for k in range(16):
-        for group in range(2):
-            ux[(3 + k) * 32 + group * 8 : (3 + k) * 32 + group * 8 + 8, :] = us[
-                pl.ds(group * 128 + k, 8, stride=16), :
-            ]
-        ux[(3 + k) * 32 + 16 : (3 + k) * 32 + 20, :] = us[pl.ds(256 + k, 4, stride=16), :]
-    for k in range(8):
-        row = cp[pl.ds(k, 5, stride=8), :]
-        ux[(3 + k) * 32 + 24 : (3 + k) * 32 + 29, :] = row
-        ux[(11 + k) * 32 + 24 : (11 + k) * 32 + 29, :] = row
-
-    for t in range(2):
-        ty[t, 8:136, :] = us[t * 128 : t * 128 + 128, :].T
-        ty[3 + t, 8:136, :] = fy[t * 128 : t * 128 + 128, :].T
-    tail = us[256:320, :]
-    ty[2, 8:136, :] = jnp.concatenate([tail, tail], axis=0).T
-    tail = fy[256:320, :]
-    ty[5, 8:136, :] = jnp.concatenate([tail, tail], axis=0).T
-    for f, entry in enumerate(flux_entries(coarse, coarse_inverse, coarse_pressure, 2)):
-        fcp[f * 8 : f * 8 + 8, :] = entry
-    for t, ref in ((6, cp), (7, fcp)):
-        both = ref[0:40, :]
-        swapped = swap_halves(both)
-        front = jnp.where(first_half_40, both, swapped)
-        back = jnp.where(first_half_40, swapped, both)
-        ty[t, 8:136, :] = jnp.concatenate([front, front[0:24], back, back[0:24]], axis=0).T
-
     pl.semaphore_wait(barrier, len(greeted))
     next_z, last_z = near((0, 1)), near((0, GZ - 1))
     next_x, last_x = along(1), along(GX - 1)
@@ -263,14 +239,6 @@
         send(5, pk.at[:, pl.ds(8, 8)], hb.at[1, :, pl.ds(0, 8)], corner(CORNERS[1])),
         send(6, pk.at[:, pl.ds(0, 8)], hb.at[0, :, pl.ds(24, 8)], corner(CORNERS[2])),
         send(7, pk.at[:, pl.ds(0, 8)], hb.at[1, :, pl.ds(24, 8)], corner(CORNERS[3])),
-    ]
-    state_x = [
-        send(8, ux.at[pl.ds(16 * 32, 96)], ux.at[pl.ds(0, 96)], next_x),
-        send(9, ux.at[pl.ds(3 * 32, 96)], ux.at[pl.ds(19 * 32, 96)], last_x),
-    ]
-    state_y = [
-        send(10, ty.at[:, pl.ds(128, 8)], ty.at[:, pl.ds(0, 8)], next_y),
-        send(11, ty.at[:, pl.ds(8, 8)], ty.at[:, pl.ds(136, 8)], last_y),
     ]
     state_z = [
         send(12, uz.at[:, pl.ds(4, 3)], uz.at[:, pl.ds(0, 3)], next_z),
@@ -299,6 +267,42 @@
         return copies, whole
 
     state_column, state_column_sent = column(gs, gs_send, gs_recv)
+
+    for k in range(16):
+        for group in range(2):
+            ux[(3 + k) * 32 + group * 8 : (3 + k) * 32 + group * 8 + 8, :] = us[
+                pl.ds(group * 128 + k, 8, stride=16), :
+            ]
+        ux[(3 + k) * 32 + 16 : (3 + k) * 32 + 20, :] = us[pl.ds(256 + k, 4, stride=16), :]
+    for k in range(8):
+        row = cp[pl.ds(k, 5, stride=8), :]
+        ux[(3 + k) * 32 + 24 : (3 + k) * 32 + 29, :] = row
+        ux[(11 + k) * 32 + 24 : (11 + k) * 32 + 29, :] = row
+
+    state_x = [
+        send(8, ux.at[pl.ds(16 * 32, 96)], ux.at[pl.ds(0, 96)], next_x),
+        send(9, ux.at[pl.ds(3 * 32, 96)], ux.at[pl.ds(19 * 32, 96)], last_x),
+    ]
+
+    for t in range(2):
+        ty[t, 8:136, :] = us[t * 128 : t * 128 + 128, :].T
+        ty[3 + t, 8:136, :] = fy[t * 128 : t * 128 + 128, :].T
+    tail = us[256:320, :]
+    ty[2, 8:136, :] = jnp.concatenate([tail, tail], axis=0).T
+    tail = fy[256:320, :]
+    ty[5, 8:136, :] = jnp.concatenate([tail, tail], axis=0).T
+    for f, entry in enumerate(flux_entries(coarse, coarse_inverse, coarse_pressure, 2)):
+        fcp[f * 8 : f * 8 + 8, :] = entry
+    for t, ref in ((6, cp), (7, fcp)):
+        both = ref[0:40, :]
+        swapped = swap_halves(both)
+        front = jnp.where(first_half_40, both, swapped)
+        back = jnp.where(first_half_40, swapped, both)
+        ty[t, 8:136, :] = jnp.concatenate([front, front[0:24], back, back[0:24]], axis=0).T
+    state_y = [
+        send(10, ty.at[:, pl.ds(128, 8)], ty.at[:, pl.ds(0, 8)], next_y),
+        send(11, ty.at[:, pl.ds(8, 8)], ty.at[:, pl.ds(136, 8)], last_y),
+    ]
 
     def flux_x(k, carry):
         base = k * 32
@@ -493,6 +497,45 @@
             for k in range(6):
                 d1[n, f, k] = planes[k + 1] - planes[k]
 
+    second_round = total_wait(sp2, 15, s2_send, s2_recv)
+    second_round.wait_recv()
+    speeds = jnp.max(sp2[...], axis=0, keepdims=True)
+    front_row = lax.broadcasted_iota(jnp.int32, (1, 128), 1) < 64
+    speed_fine = jnp.broadcast_to(
+        jnp.max(jnp.where(front_row, speeds, 0.0), axis=1, keepdims=True), (8, 128)
+    )
+    speed_coarse = jnp.broadcast_to(
+        jnp.max(jnp.where(front_row, 0.0, speeds), axis=1, keepdims=True), (8, 128)
+    )
+
+    def sweep_16(g, carry):
+        out = sweep([d16[0, g, k] for k in range(21)], [d16[1, g, k] for k in range(21)], speed_fine, 16)
+        for k in range(16):
+            a16[pl.ds(g * 128 + k, 8, stride=16), :] = out[k]
+        return carry
+
+    def sweep_4(g, carry):
+        out = sweep([dz[0, g, k] for k in range(9)], [dz[1, g, k] for k in range(9)], speed_fine, 4)
+        for z in range(4):
+            az[g, z] = out[z]
+        return carry
+
+    def sweep_8(g, carry):
+        out = sweep([d8[0, g, k] for k in range(13)], [d8[1, g, k] for k in range(13)], speed_coarse, 8)
+        for k in range(8):
+            a8[pl.ds(g * 64 + k, 8, stride=8), :] = out[k]
+        return carry
+
+    def sweep_1(g, carry):
+        out = sweep([d1[0, g, k] for k in range(6)], [d1[1, g, k] for k in range(6)], speed_coarse, 1)
+        a1[g] = out[0]
+        return carry
+
+    lax.fori_loop(0, 6, sweep_16, 0)
+    lax.fori_loop(0, 10, sweep_4, 0)
+    lax.fori_loop(0, 2, sweep_8, 0)
+    lax.fori_loop(0, 5, sweep_1, 0)
+
     for copy in noise_z:
         copy.wait_recv()
     for h in range(2):
@@ -531,45 +574,6 @@
     coarse_source = [None, coarse[0] * push[0], coarse[0] * push[1], coarse[0] * push[2], work]
     for f in range(1, 5):
         fcp[f * 8 : f * 8 + 8, :] = coarse_source[f]
-
-    second_round = total_wait(sp2, 15, s2_send, s2_recv)
-    second_round.wait_recv()
-    speeds = jnp.max(sp2[...], axis=0, keepdims=True)
-    front_row = lax.broadcasted_iota(jnp.int32, (1, 128), 1) < 64
-    speed_fine = jnp.broadcast_to(
-        jnp.max(jnp.where(front_row, speeds, 0.0), axis=1, keepdims=True), (8, 128)
-    )
-    speed_coarse = jnp.broadcast_to(
-        jnp.max(jnp.where(front_row, 0.0, speeds), axis=1, keepdims=True), (8, 128)
-    )
-
-    def sweep_16(g, carry):
-        out = sweep([d16[0, g, k] for k in range(21)], [d16[1, g, k] for k in range(21)], speed_fine, 16)
-        for k in range(16):
-            a16[pl.ds(g * 128 + k, 8, stride=16), :] = out[k]
-        return carry
-
-    def sweep_4(g, carry):
-        out = sweep([dz[0, g, k] for k in range(9)], [dz[1, g, k] for k in range(9)], speed_fine, 4)
-        for z in range(4):
-            az[g, z] = out[z]
-        return carry
-
-    def sweep_8(g, carry):
-        out = sweep([d8[0, g, k] for k in range(13)], [d8[1, g, k] for k in range(13)], speed_coarse, 8)
-        for k in range(8):
-            a8[pl.ds(g * 64 + k, 8, stride=8), :] = out[k]
-        return carry
-
-    def sweep_1(g, carry):
-        out = sweep([d1[0, g, k] for k in range(6)], [d1[1, g, k] for k in range(6)], speed_coarse, 1)
-        a1[g] = out[0]
-        return carry
-
-    lax.fori_loop(0, 6, sweep_16, 0)
-    lax.fori_loop(0, 10, sweep_4, 0)
-    lax.fori_loop(0, 2, sweep_8, 0)
-    lax.fori_loop(0, 5, sweep_1, 0)
 
     rate_fine = 0.1 / speed_fine
     rate_coarse = 0.1 / speed_coarse

time: 33.7 us -> 31.6 us (0.938)
  Pallas kernels: 31.4 us -> 29.4 us
    pallas_call x1, Pallas kernels: 31.4 us -> 29.4 us  [local(): pl.pallas_call(kernel, out_shape=(jax.ShapeDtypeStruct((320, 128), f32),...]
where the time goes in v3:
time: 31.6 us; the launch traced here: 31.4 us
  Pallas kernels  29.4 us (93%)
  other arithmetic  1.32 us (4%)
  between operations  0.66 us (2%)
    pallas_call x1, Pallas kernels, local(): pl.pallas_call(kernel, out_shape=(jax.ShapeDtypeStruct((320, 128), f32),...  29.4 us
    add x1, other arithmetic, local(): 0.75 * fine_start + fine.reshape(fine_start.shape)  0.7 us

profile of v3, /device:TPU:1, one launch (start us, length us, event | category | flops | bytes accessed | tf_op | source)
XLA Modules:
  0.0 31.4 jit_solution(16042871232854601417)
XLA Ops:
  0.6 0.0 copy-start
  0.6 29.4 %section.1 = (f32[320,128]{1,0:T(8,128)S(1)}, f32[80,64]{1,0:T(8,128)S(1)}) custom-call(f32[320,128]{1,0:T(8,128)} %bitcast.7, f32[192,128]{1,0:T(8,128)} %bitcast.8, f32[80,64]{1,0:T(8,128)} %bitcast.9, f32[3,9]{1,0:T(4,128)} %taps_hbm.1, s32[8]{0:T(128)} %owner_hbm.1), custom_call_target="tpu_custom_call" | custom-call | tf_op jit(solution)/shard_map/section/pallas_call | solution.py:615
  30.0 0.0 copy-done
  30.0 0.0 copy-start.1
  30.0 0.7 %multiply_add_fusion = f32[5,4,16,128]{3,2,1,0:T(8,128)} fusion(f32[5,4,16,128]{3,2,1,0:T(8,128)S(1)} %bitcast.5, f32[5,4,16,128]{3,2,1,0:T(8,128)S(1)} %copy-done), kind=kLoop, calls=%fused_computation | loop fusion | flops 81920 | bytes 491520 | tf_op jit(solution)/shard_map/add | solution.py:672
  30.7 0.1 copy-done.1
  30.8 0.6 %multiply_add_fusion.1 = f32[5,2,8,64]{3,2,1,0:T(8,128)} fusion(f32[5,2,8,64]{3,2,1,0:T(8,128)S(1)} %bitcast.6, f32[5,2,8,64]{3,2,1,0:T(8,128)S(1)} %copy-done.1), kind=kLoop, calls=%fused_computation.1 | loop fusion | flops 10240 | bytes 61440 | tf_op jit(solution)/shard_map/add | solution.py:673
Async XLA Ops:
  0.6 29.4 %copy-start = (f32[5,4,16,128]{3,2,1,0:T(8,128)S(1)}, f32[5,4,16,128]{3,2,1,0:T(8,128)}, u32[]{:S(2)}) copy-start(f32[5,4,16,128]{3,2,1,0:T(8,128)} %param.7) | copy-start | bytes 491524
  30.0 0.8 %copy-start.1 = (f32[5,2,8,64]{3,2,1,0:T(8,128)S(1)}, f32[5,2,8,64]{3,2,1,0:T(8,128)}, u32[]{:S(2)}) copy-start(f32[5,2,8,64]{3,2,1,0:T(8,128)} %param.10) | copy-start | bytes 61444

commit v4 on v3

--- a/solution.py
+++ b/solution.py
@@ -8,7 +8,7 @@
 MESH = pl.DeviceIdType.MESH
 GX, GY, GZ = 16, 4, 8
 GAMMA = 1.4
-SPEED_EPS = 3e-06
+INDICATOR_EPS = 2e-06
 RESTRICT_SCALE = 0.35355339059327373
 NEAR = sorted(
     ((i, j) for i in range(GY) for j in range(GZ) if (i, j) != (0, 0)),
@@ -47,47 +47,61 @@
     return largest * inverse + jnp.sqrt(GAMMA * pressure * inverse)
 
 
-def side(low, mid, high, p, q, r, s):
-    m0 = mid * high
-    m1 = low * high
-    m2 = low * mid
-    w0 = m0 * m0
-    w1 = 6.0 * (m1 * m1)
-    w2 = 3.0 * (m2 * m2)
-    total = w0 + w1 + w2
-    sums = w0 * (5.0 * q - 2.0 * p) + w1 * (q + 2.0 * r) + w2 * (4.0 * r - s)
-    guess = pl.reciprocal(total, approx=True)
-    return sums * (guess * (2.0 - total * guess))
+def prepare(steps, flux):
+    cells = len(steps) - 5
+    bends = [steps[k - 1] - 2.0 * steps[k] + steps[k + 1] for k in range(1, cells + 4)]
+    if flux:
+        linear = [
+            steps[c + 2] + steps[c + 3] + (steps[c + 2] - steps[c + 4] - steps[c + 1] + steps[c + 3]) * (1.0 / 6.0)
+            for c in range(cells)
+        ]
+    else:
+        linear = [
+            steps[c + 2] - steps[c + 3]
+            + (steps[c + 4] - steps[c + 1] + 3.0 * (steps[c + 3] - steps[c + 2])) * (1.0 / 6.0)
+            for c in range(cells)
+        ]
+    return list(steps) + bends + linear
 
 
 def indicators(steps):
     squares = [e * e for e in steps]
+    raised = [(2.0 / 3.0) * x + 0.5 * INDICATOR_EPS for x in squares]
     low, mid, high = [], [], []
     for i in range(len(steps) - 1):
         cross = steps[i] * steps[i + 1]
-        both = squares[i] + squares[i + 1] + SPEED_EPS
-        base = both - 2.75 * cross
-        low.append(base + 1.5 * squares[i + 1])
-        high.append(base + 1.5 * squares[i])
-        mid.append(both - 1.25 * cross)
+        base = raised[i] + raised[i + 1] - (11.0 / 6.0) * cross
+        low.append(base + squares[i + 1])
+        high.append(base + squares[i])
+        mid.append(base + cross)
     return low, mid, high
 
 
-def sweep(flux_steps, state_steps, speed, cells):
-    scaled = [speed * u for u in state_steps]
-    up = [f + u for f, u in zip(flux_steps, scaled)]
-    down = [f - u for f, u in zip(flux_steps, scaled)]
-    low_u, mid_u, high_u = indicators(up)
+def side(low, mid, high, first, second):
+    to_mid = low * pltpu.reciprocal(mid, approx=True)
+    to_high = low * pltpu.reciprocal(high, approx=True)
+    w2 = 1.5 * (to_high * to_high)
+    total = 3.0 * (to_mid * to_mid) + w2 + 0.5
+    return (first + w2 * second) * pltpu.reciprocal(total, approx=True)
+
+
+def sweep(flux, state, speed, cells):
+    steps, bends = cells + 5, cells + 3
+    scaled = [speed * u for u in state]
+    up = [f + u for f, u in zip(flux[:steps], scaled[:steps])]
+    down = [f - u for f, u in zip(flux[:steps], scaled[:steps])]
+    low_u, mid_u, high_u = indicators(up[: cells + 4])
     low_d, mid_d, high_d = indicators(down)
+    bend_u = [f + u for f, u in zip(flux[steps : steps + bends], scaled[steps : steps + bends])]
+    bend_d = [f - u for f, u in zip(flux[steps : steps + bends], scaled[steps : steps + bends])]
     faces = []
     for j in range(cells + 1):
-        right = side(low_u[j], mid_u[j + 1], high_u[j + 2], up[j], up[j + 1], up[j + 2], up[j + 3])
-        left = side(
-            high_d[j + 3], mid_d[j + 2], low_d[j + 1], down[j + 4], down[j + 3], down[j + 2], down[j + 1]
-        )
-        faces.append(right - left)
+        right = side(low_u[j], mid_u[j + 1], high_u[j + 2], bend_u[j], bend_u[j + 1])
+        left = side(high_d[j + 3], mid_d[j + 2], low_d[j + 1], bend_d[j + 2], bend_d[j + 1])
+        faces.append(left - right)
     return [
-        up[c + 2] + down[c + 3] + (faces[c + 1] - faces[c]) * (1.0 / 6.0) for c in range(cells)
+        flux[steps + bends + c] + scaled[steps + bends + c] + (faces[c + 1] - faces[c]) * (1.0 / 6.0)
+        for c in range(cells)
     ]
 
 
@@ -98,7 +112,7 @@
 def kernel(
     us_hbm, noise_hbm, cs_hbm, taps_hbm, owner_hbm, fine_out, coarse_out,
     us, noise, cs, taps, owner, sp1, sp2, cp, fcp, ux, fx, ty, fy, uz, fz, nz, gs, gr, nx, pk, hb, wx, nt,
-    force, halves, dz, d16, d8, d1, az, a16, a8, a1,
+    force, halves, dz, d16, d8, d1, az, a16, ay, a8, a1,
     ins, far_sem, s1_send, s1_recv, s2_send, s2_recv, gs_send, gs_recv, gr_send, gr_recv, hs, hr,
 ):
     loads = [
@@ -129,19 +143,15 @@
     first_half = lane < 64
     first_half_40 = lax.broadcasted_iota(jnp.int32, (40, 128), 1) < 64
 
+    def cells(z):
+        return [us[(f * 4 + z) * 16 : (f * 4 + z) * 16 + 16, :] for f in range(5)]
+
     loads[0].wait()
     best = jnp.zeros((16, 128), jnp.float32)
     for z in range(4):
-        state = [us[(f * 4 + z) * 16 : (f * 4 + z) * 16 + 16, :] for f in range(5)]
+        state = cells(z)
         inverse = 1.0 / state[0]
-        pressure = pressure_of(state, inverse)
-        best = jnp.maximum(best, fastest_of(state, inverse, pressure))
-        for f, entry in enumerate(flux_entries(state, inverse, pressure, 2)):
-            fy[(f * 4 + z) * 16 : (f * 4 + z) * 16 + 16, :] = entry
-        for f, entry in enumerate(flux_entries(state, inverse, pressure, 3)):
-            fz[f, 3 + z] = entry
-        for f in range(5):
-            uz[f, 3 + z] = state[f]
+        best = jnp.maximum(best, fastest_of(state, inverse, pressure_of(state, inverse)))
     best = jnp.maximum(best[0:8], best[8:16])
     loads[1].wait()
     for f in range(5):
@@ -158,6 +168,27 @@
         jnp.maximum(coarse_best, swap_halves(coarse_best)),
     )
     sp1[31:32, :] = jnp.max(best, axis=0, keepdims=True)
+
+    pl.semaphore_wait(barrier, len(greeted))
+    next_z, last_z = near((0, 1)), near((0, GZ - 1))
+    next_x, last_x = along(1), along(GX - 1)
+    next_y, last_y = near((1, 0)), near((GY - 1, 0))
+
+    def send(index, src, dst, device):
+        copy = pltpu.make_async_remote_copy(
+            src_ref=src, dst_ref=dst, send_sem=hs.at[index], recv_sem=hr.at[index],
+            device_id=device, device_id_type=MESH,
+        )
+        copy.start()
+        return copy
+
+    for n, step in enumerate(NEAR):
+        pltpu.make_async_remote_copy(
+            src_ref=sp1.at[pl.ds(31, 1)], dst_ref=sp1.at[pl.ds(n, 1)], send_sem=s1_send,
+            recv_sem=s1_recv, device_id=near(step), device_id_type=MESH,
+        ).start()
+    for step in (4, GX - 4):
+        pl.semaphore_signal(far_sem, inc=1, device_id=along(step), device_id_type=MESH)
 
     for load in loads[2:]:
         load.wait()
@@ -210,26 +241,6 @@
     for f in range(5):
         gs[gz, f] = coarse[f]
 
-    pl.semaphore_wait(barrier, len(greeted))
-    next_z, last_z = near((0, 1)), near((0, GZ - 1))
-    next_x, last_x = along(1), along(GX - 1)
-    next_y, last_y = near((1, 0)), near((GY - 1, 0))
-
-    def send(index, src, dst, device):
-        copy = pltpu.make_async_remote_copy(
-            src_ref=src, dst_ref=dst, send_sem=hs.at[index], recv_sem=hr.at[index],
-            device_id=device, device_id_type=MESH,
-        )
-        copy.start()
-        return copy
-
-    for n, step in enumerate(NEAR):
-        pltpu.make_async_remote_copy(
-            src_ref=sp1.at[pl.ds(31, 1)], dst_ref=sp1.at[pl.ds(n, 1)], send_sem=s1_send,
-            recv_sem=s1_recv, device_id=near(step), device_id_type=MESH,
-        ).start()
-    for step in (4, GX - 4):
-        pl.semaphore_signal(far_sem, inc=1, device_id=along(step), device_id_type=MESH)
     noise_xy = [
         send(0, nx.at[:, pl.ds(16, 8)], nx.at[:, pl.ds(0, 8)], next_x),
         send(1, nx.at[:, pl.ds(8, 8)], nx.at[:, pl.ds(24, 8)], last_x),
@@ -240,6 +251,18 @@
         send(6, pk.at[:, pl.ds(0, 8)], hb.at[0, :, pl.ds(24, 8)], corner(CORNERS[2])),
         send(7, pk.at[:, pl.ds(0, 8)], hb.at[1, :, pl.ds(24, 8)], corner(CORNERS[3])),
     ]
+
+    for z in range(4):
+        state = cells(z)
+        inverse = 1.0 / state[0]
+        pressure = pressure_of(state, inverse)
+        for f, entry in enumerate(flux_entries(state, inverse, pressure, 2)):
+            fy[(f * 4 + z) * 16 : (f * 4 + z) * 16 + 16, :] = entry
+        for f, entry in enumerate(flux_entries(state, inverse, pressure, 3)):
+            fz[f, 3 + z] = entry
+        for f in range(5):
+            uz[f, 3 + z] = state[f]
+
     state_z = [
         send(12, uz.at[:, pl.ds(4, 3)], uz.at[:, pl.ds(0, 3)], next_z),
         send(13, uz.at[:, pl.ds(3, 3)], uz.at[:, pl.ds(7, 3)], last_z),
@@ -425,27 +448,26 @@
     for k in (11, 12, 13):
         ux[k * 32 + 24 : k * 32 + 32, :] = ux[(k + 8) * 32 + 24 : (k + 8) * 32 + 32, :]
 
-    def steps_x(k, carry):
-        for n, ref in enumerate((fx, ux)):
-            for group in range(3):
-                d16[n, group, k] = ref[pl.ds((k + 1) * 32 + group * 8, 8), :] - ref[
-                    pl.ds(k * 32 + group * 8, 8), :
-                ]
-        return carry
-
-    lax.fori_loop(0, 21, steps_x, 0)
+    def store(ref, n, group, rows):
+        for k, value in enumerate(prepare([rows[k + 1] - rows[k] for k in range(len(rows) - 1)], n == 0)):
+            ref[n, group, k] = value
+
     for n, ref in enumerate((fx, ux)):
-        for k in range(13):
-            d8[n, 0, k] = ref[(k + 1) * 32 + 24 : (k + 1) * 32 + 32, :] - ref[k * 32 + 24 : k * 32 + 32, :]
+
+        def steps_x(group, carry):
+            base = pl.multiple_of(group * 8, 8)
+            store(d16, n, group, [ref[pl.ds(k * 32 + base, 8), :] for k in range(22)])
+            return carry
+
+        lax.fori_loop(0, 3, steps_x, 0)
+        store(d8, n, 0, [ref[k * 32 + 24 : k * 32 + 32, :] for k in range(14)])
 
     for copy in state_y:
         copy.wait_recv()
     for n in range(2):
 
         def steps_y(t, carry):
-            rows = [ty[3 - 3 * n + t, pl.ds(5 + k, 8, stride=16), :] for k in range(22)]
-            for k in range(21):
-                d16[n, 3 + t, k] = rows[k + 1] - rows[k]
+            store(d16, n, 3 + t, [ty[3 - 3 * n + t, pl.ds(5 + k, 8, stride=16), :] for k in range(22)])
             return carry
 
         lax.fori_loop(0, 3, steps_y, 0)
@@ -453,9 +475,7 @@
         copy.wait_send()
     for n, t in enumerate((7, 6)):
         ty[t, 72:80, :] = ty[t, 136:144, :]
-        rows = [ty[t, pl.ds(5 + k, 8, stride=8), :] for k in range(14)]
-        for k in range(13):
-            d8[n, 1, k] = rows[k + 1] - rows[k]
+        store(d8, n, 1, [ty[t, pl.ds(5 + k, 8, stride=8), :] for k in range(14)])
 
     for copy in state_z:
         copy.wait_recv()
@@ -467,9 +487,7 @@
     def steps_z(f, carry):
         for n, ref in enumerate((fz, uz)):
             for h in range(2):
-                for k in range(9):
-                    d4 = ref[f, k + 1, h * 8 : h * 8 + 8, :] - ref[f, k, h * 8 : h * 8 + 8, :]
-                    dz[n, f * 2 + h, k] = d4
+                store(dz, n, f * 2 + h, [ref[f, k, h * 8 : h * 8 + 8, :] for k in range(10)])
         return carry
 
     lax.fori_loop(0, 5, steps_z, 0)
@@ -494,8 +512,7 @@
             for j in range(-3, 4):
                 m = (j + 4) // 2
                 planes.append(pairs[m][f] if j % 2 == 0 else mixed(pairs[m][f], pairs[m + 1][f]))
-            for k in range(6):
-                d1[n, f, k] = planes[k + 1] - planes[k]
+            store(d1, n, f, planes)
 
     second_round = total_wait(sp2, 15, s2_send, s2_recv)
     second_round.wait_recv()
@@ -508,31 +525,40 @@
         jnp.max(jnp.where(front_row, 0.0, speeds), axis=1, keepdims=True), (8, 128)
     )
 
-    def sweep_16(g, carry):
-        out = sweep([d16[0, g, k] for k in range(21)], [d16[1, g, k] for k in range(21)], speed_fine, 16)
-        for k in range(16):
-            a16[pl.ds(g * 128 + k, 8, stride=16), :] = out[k]
-        return carry
-
-    def sweep_4(g, carry):
-        out = sweep([dz[0, g, k] for k in range(9)], [dz[1, g, k] for k in range(9)], speed_fine, 4)
-        for z in range(4):
-            az[g, z] = out[z]
+    def taken(ref, n, g, cells):
+        return [ref[n, g, k] for k in range(3 * cells + 8)]
+
+    def sweep_16(g):
+        for k, out in enumerate(sweep(taken(d16, 0, g, 16), taken(d16, 1, g, 16), speed_fine, 16)):
+            a16[pl.ds(g * 128 + k, 8, stride=16), :] = out
+
+    def sweep_y(g, carry):
+        sweep_16(3 + g)
+        return carry
+
+    def sweep_x(g, carry):
+        sweep_16(g)
+        row = pl.multiple_of(g * 128, 128)
+        ay[pl.ds(row, 128), :] = a16[pl.ds(384 + row, 128), :].T
+        return carry
+
+    def sweep_z(g, carry):
+        for z, out in enumerate(sweep(taken(dz, 0, g, 4), taken(dz, 1, g, 4), speed_fine, 4)):
+            az[g, z] = out
         return carry
 
     def sweep_8(g, carry):
-        out = sweep([d8[0, g, k] for k in range(13)], [d8[1, g, k] for k in range(13)], speed_coarse, 8)
-        for k in range(8):
-            a8[pl.ds(g * 64 + k, 8, stride=8), :] = out[k]
+        for k, out in enumerate(sweep(taken(d8, 0, g, 8), taken(d8, 1, g, 8), speed_coarse, 8)):
+            a8[pl.ds(g * 64 + k, 8, stride=8), :] = out
         return carry
 
     def sweep_1(g, carry):
-        out = sweep([d1[0, g, k] for k in range(6)], [d1[1, g, k] for k in range(6)], speed_coarse, 1)
-        a1[g] = out[0]
-        return carry
-
-    lax.fori_loop(0, 6, sweep_16, 0)
-    lax.fori_loop(0, 10, sweep_4, 0)
+        a1[g] = sweep(taken(d1, 0, g, 1), taken(d1, 1, g, 1), speed_coarse, 1)[0]
+        return carry
+
+    lax.fori_loop(0, 3, sweep_y, 0)
+    lax.fori_loop(0, 3, sweep_x, 0)
+    lax.fori_loop(0, 10, sweep_z, 0)
     lax.fori_loop(0, 2, sweep_8, 0)
     lax.fori_loop(0, 5, sweep_1, 0)
 
@@ -577,16 +603,13 @@
 
     rate_fine = 0.1 / speed_fine
     rate_coarse = 0.1 / speed_coarse
-    for t in range(3):
-        wide = a16[384 + t * 128 : 512 + t * 128, :].T
-        for tile in range(16 if t < 2 else 8):
-            index = t * 16 + tile
-            f, z, h = index // 8, (index // 2) % 4, index % 2
-            row = index * 8
-            change = -0.5 * (a16[row : row + 8, :] + wide[tile * 8 : tile * 8 + 8] + az[f * 2 + h, z])
-            if f > 0:
-                change = change + force[(f - 1) * 4 + z, h * 8 : h * 8 + 8, :]
-            fine_out[row : row + 8, :] = 0.25 * us[row : row + 8, :] + rate_fine * change
+    for index in range(40):
+        f, z, h = index // 8, (index // 2) % 4, index % 2
+        row = index * 8
+        change = -0.5 * (a16[row : row + 8, :] + ay[row : row + 8, :] + az[f * 2 + h, z])
+        if f > 0:
+            change = change + force[(f - 1) * 4 + z, h * 8 : h * 8 + 8, :]
+        fine_out[row : row + 8, :] = 0.25 * us[row : row + 8, :] + rate_fine * change
 
     along_y = a8[64:128, :]
     turned = jnp.concatenate([along_y, along_y], axis=0).T
@@ -643,12 +666,13 @@
             pltpu.VMEM((2, 144, 128), f32),
             pltpu.VMEM((16, 16, 128), f32),
             pltpu.VMEM((96, 128), f32),
-            pltpu.VMEM((2, 10, 9, 8, 128), f32),
-            pltpu.VMEM((2, 6, 21, 8, 128), f32),
-            pltpu.VMEM((2, 2, 13, 8, 128), f32),
-            pltpu.VMEM((2, 5, 6, 8, 128), f32),
+            pltpu.VMEM((2, 10, 20, 8, 128), f32),
+            pltpu.VMEM((2, 6, 56, 8, 128), f32),
+            pltpu.VMEM((2, 2, 32, 8, 128), f32),
+            pltpu.VMEM((2, 5, 11, 8, 128), f32),
             pltpu.VMEM((10, 4, 8, 128), f32),
             pltpu.VMEM((768, 128), f32),
+            pltpu.VMEM((384, 128), f32),
             pltpu.VMEM((128, 128), f32),
             pltpu.VMEM((5, 8, 128), f32),
             dma((5,)),

time: 31.6 us -> 31.3 us (level)
  Pallas kernels: 29.4 us -> 29 us
    pallas_call x1, Pallas kernels: 29.4 us -> 29 us  [local(): pl.pallas_call(kernel, out_shape=(jax.ShapeDtypeStruct((320, 128), f32),...]
where the time goes in v4:
time: 31.3 us; the launch traced here: 31.1 us
  Pallas kernels  29 us (93%)
  other arithmetic  1.32 us (4%)
  between operations  0.66 us (2%)
    pallas_call x1, Pallas kernels, local(): pl.pallas_call(kernel, out_shape=(jax.ShapeDtypeStruct((320, 128), f32),...  29 us
    add x1, other arithmetic, local(): 0.75 * fine_start + fine.reshape(fine_start.shape)  0.7 us

profile of v4, /device:TPU:1, one launch (start us, length us, event | category | flops | bytes accessed | tf_op | source)
XLA Modules:
  0.0 31.1 jit_solution(6136211273969804165)
XLA Ops:
  0.6 0.0 copy-start
  0.6 29.0 %section.1 = (f32[320,128]{1,0:T(8,128)S(1)}, f32[80,64]{1,0:T(8,128)S(1)}) custom-call(f32[320,128]{1,0:T(8,128)} %bitcast.7, f32[192,128]{1,0:T(8,128)} %bitcast.8, f32[80,64]{1,0:T(8,128)} %bitcast.9, f32[3,9]{1,0:T(4,128)} %taps_hbm.1, s32[8]{0:T(128)} %owner_hbm.1), custom_call_target="tpu_custom_call" | custom-call | tf_op jit(solution)/shard_map/section/pallas_call | solution.py:638
  29.6 0.0 copy-done
  29.7 0.0 copy-start.1
  29.7 0.7 %multiply_add_fusion = f32[5,4,16,128]{3,2,1,0:T(8,128)} fusion(f32[5,4,16,128]{3,2,1,0:T(8,128)S(1)} %bitcast.5, f32[5,4,16,128]{3,2,1,0:T(8,128)S(1)} %copy-done), kind=kLoop, calls=%fused_computation | loop fusion | flops 81920 | bytes 491520 | tf_op jit(solution)/shard_map/add | solution.py:696
  30.4 0.1 copy-done.1
  30.4 0.6 %multiply_add_fusion.1 = f32[5,2,8,64]{3,2,1,0:T(8,128)} fusion(f32[5,2,8,64]{3,2,1,0:T(8,128)S(1)} %bitcast.6, f32[5,2,8,64]{3,2,1,0:T(8,128)S(1)} %copy-done.1), kind=kLoop, calls=%fused_computation.1 | loop fusion | flops 10240 | bytes 61440 | tf_op jit(solution)/shard_map/add | solution.py:697
Async XLA Ops:
  0.6 29.0 %copy-start = (f32[5,4,16,128]{3,2,1,0:T(8,128)S(1)}, f32[5,4,16,128]{3,2,1,0:T(8,128)}, u32[]{:S(2)}) copy-start(f32[5,4,16,128]{3,2,1,0:T(8,128)} %param.7) | copy-start | bytes 491524
  29.7 0.8 %copy-start.1 = (f32[5,2,8,64]{3,2,1,0:T(8,128)S(1)}, f32[5,2,8,64]{3,2,1,0:T(8,128)}, u32[]{:S(2)}) copy-start(f32[5,2,8,64]{3,2,1,0:T(8,128)} %param.10) | copy-start | bytes 61444

commit v5 on v4

--- a/solution.py
+++ b/solution.py
@@ -542,25 +542,23 @@
         ay[pl.ds(row, 128), :] = a16[pl.ds(384 + row, 128), :].T
         return carry
 
-    def sweep_z(g, carry):
+    def sweep_z(g):
         for z, out in enumerate(sweep(taken(dz, 0, g, 4), taken(dz, 1, g, 4), speed_fine, 4)):
             az[g, z] = out
+
+    def sweep_five(half, carry):
+        for n in range(5):
+            sweep_z(half * 5 + n)
         return carry
 
-    def sweep_8(g, carry):
+    lax.fori_loop(0, 3, sweep_y, 0)
+    lax.fori_loop(0, 3, sweep_x, 0)
+    lax.fori_loop(0, 2, sweep_five, 0)
+    for g in range(2):
         for k, out in enumerate(sweep(taken(d8, 0, g, 8), taken(d8, 1, g, 8), speed_coarse, 8)):
             a8[pl.ds(g * 64 + k, 8, stride=8), :] = out
-        return carry
-
-    def sweep_1(g, carry):
+    for g in range(5):
         a1[g] = sweep(taken(d1, 0, g, 1), taken(d1, 1, g, 1), speed_coarse, 1)[0]
-        return carry
-
-    lax.fori_loop(0, 3, sweep_y, 0)
-    lax.fori_loop(0, 3, sweep_x, 0)
-    lax.fori_loop(0, 10, sweep_z, 0)
-    lax.fori_loop(0, 2, sweep_8, 0)
-    lax.fori_loop(0, 5, sweep_1, 0)
 
     for copy in noise_z:
         copy.wait_recv()

time: 31.3 us -> 31.3 us (level)
  no operation moved by 1% of the time
where the time goes in v5:
time: 31.3 us; the launch traced here: 31.1 us
  Pallas kernels  29 us (93%)
  other arithmetic  1.32 us (4%)
  between operations  0.66 us (2%)
    pallas_call x1, Pallas kernels, local(): pl.pallas_call(kernel, out_shape=(jax.ShapeDtypeStruct((320, 128), f32),...  29 us
    add x1, other arithmetic, local(): 0.75 * fine_start + fine.reshape(fine_start.shape)  0.7 us

profile of v5, /device:TPU:1, one launch (start us, length us, event | category | flops | bytes accessed | tf_op | source)
XLA Modules:
  0.0 31.1 jit_solution(9585927989933834121)
XLA Ops:
  0.6 0.0 copy-start
  0.6 29.0 %section.1 = (f32[320,128]{1,0:T(8,128)S(1)}, f32[80,64]{1,0:T(8,128)S(1)}) custom-call(f32[320,128]{1,0:T(8,128)} %bitcast.7, f32[192,128]{1,0:T(8,128)} %bitcast.8, f32[80,64]{1,0:T(8,128)} %bitcast.9, f32[3,9]{1,0:T(4,128)} %taps_hbm.1, s32[8]{0:T(128)} %owner_hbm.1), custom_call_target="tpu_custom_call" | custom-call | tf_op jit(solution)/shard_map/section/pallas_call | solution.py:636
  29.6 0.0 copy-done
  29.7 0.0 copy-start.1
  29.7 0.7 %multiply_add_fusion = f32[5,4,16,128]{3,2,1,0:T(8,128)} fusion(f32[5,4,16,128]{3,2,1,0:T(8,128)S(1)} %bitcast.5, f32[5,4,16,128]{3,2,1,0:T(8,128)S(1)} %copy-done), kind=kLoop, calls=%fused_computation | loop fusion | flops 81920 | bytes 491520 | tf_op jit(solution)/shard_map/add | solution.py:694
  30.4 0.1 copy-done.1
  30.4 0.6 %multiply_add_fusion.1 = f32[5,2,8,64]{3,2,1,0:T(8,128)} fusion(f32[5,2,8,64]{3,2,1,0:T(8,128)S(1)} %bitcast.6, f32[5,2,8,64]{3,2,1,0:T(8,128)S(1)} %copy-done.1), kind=kLoop, calls=%fused_computation.1 | loop fusion | flops 10240 | bytes 61440 | tf_op jit(solution)/shard_map/add | solution.py:695
Async XLA Ops:
  0.6 29.0 %copy-start = (f32[5,4,16,128]{3,2,1,0:T(8,128)S(1)}, f32[5,4,16,128]{3,2,1,0:T(8,128)}, u32[]{:S(2)}) copy-start(f32[5,4,16,128]{3,2,1,0:T(8,128)} %param.7) | copy-start | bytes 491524
  29.7 0.8 %copy-start.1 = (f32[5,2,8,64]{3,2,1,0:T(8,128)S(1)}, f32[5,2,8,64]{3,2,1,0:T(8,128)}, u32[]{:S(2)}) copy-start(f32[5,2,8,64]{3,2,1,0:T(8,128)} %param.10) | copy-start | bytes 61444

commit v6 on v5

--- a/solution.py
+++ b/solution.py
@@ -112,7 +112,7 @@
 def kernel(
     us_hbm, noise_hbm, cs_hbm, taps_hbm, owner_hbm, fine_out, coarse_out,
     us, noise, cs, taps, owner, sp1, sp2, cp, fcp, ux, fx, ty, fy, uz, fz, nz, gs, gr, nx, pk, hb, wx, nt,
-    force, halves, dz, d16, d8, d1, az, a16, ay, a8, a1,
+    halves, dz, d16, d8, d1, az, a16, ay, a8, a1,
     ins, far_sem, s1_send, s1_recv, s2_send, s2_recv, gs_send, gs_recv, gr_send, gr_recv, hs, hr,
 ):
     loads = [
@@ -562,28 +562,6 @@
 
     for copy in noise_z:
         copy.wait_recv()
-    for h in range(2):
-
-        def noise_along_z(c, carry):
-            planes = [nz[c, z, h * 8 : h * 8 + 8, :] for z in range(12)]
-            for z in range(4):
-                total = taps[2, 0] * planes[z]
-                for t in range(1, 9):
-                    total = total + taps[2, t] * planes[z + t]
-                force[c * 4 + z, h * 8 : h * 8 + 8, :] = total
-            return carry
-
-        lax.fori_loop(0, 3, noise_along_z, 0)
-
-    def sources(z, carry):
-        state = [us[pl.ds(pl.multiple_of((f * 4 + z) * 16, 16), 16), :] for f in range(4)]
-        push = [force[c * 4 + z] for c in range(3)]
-        for c in range(3):
-            force[c * 4 + z] = state[0] * push[c]
-        force[12 + z] = state[1] * push[0] + state[2] * push[1] + state[3] * push[2]
-        return carry
-
-    lax.fori_loop(0, 4, sources, 0)
     for copy in noise_column:
         copy.wait_recv()
     push = []
@@ -601,13 +579,24 @@
 
     rate_fine = 0.1 / speed_fine
     rate_coarse = 0.1 / speed_coarse
-    for index in range(40):
-        f, z, h = index // 8, (index // 2) % 4, index % 2
-        row = index * 8
-        change = -0.5 * (a16[row : row + 8, :] + ay[row : row + 8, :] + az[f * 2 + h, z])
-        if f > 0:
-            change = change + force[(f - 1) * 4 + z, h * 8 : h * 8 + 8, :]
-        fine_out[row : row + 8, :] = 0.25 * us[row : row + 8, :] + rate_fine * change
+    for z in range(4):
+        for h in range(2):
+            part = slice(h * 8, h * 8 + 8)
+            push = []
+            for c in range(3):
+                total = taps[2, 0] * nz[c, z, part, :]
+                for t in range(1, 9):
+                    total = total + taps[2, t] * nz[c, z + t, part, :]
+                push.append(total)
+            state = [us[(f * 4 + z) * 16 + h * 8 : (f * 4 + z) * 16 + h * 8 + 8, :] for f in range(5)]
+            work = state[1] * push[0] + state[2] * push[1] + state[3] * push[2]
+            source = [None, state[0] * push[0], state[0] * push[1], state[0] * push[2], work]
+            for f in range(5):
+                row = (f * 4 + z) * 16 + h * 8
+                change = -0.5 * (a16[row : row + 8, :] + ay[row : row + 8, :] + az[f * 2 + h, z])
+                if f > 0:
+                    change = change + source[f]
+                fine_out[row : row + 8, :] = 0.25 * state[f] + rate_fine * change
 
     along_y = a8[64:128, :]
     turned = jnp.concatenate([along_y, along_y], axis=0).T
@@ -662,7 +651,6 @@
             pltpu.VMEM((2, 2, 32, 128), f32),
             pltpu.VMEM((256, 128), f32),
             pltpu.VMEM((2, 144, 128), f32),
-            pltpu.VMEM((16, 16, 128), f32),
             pltpu.VMEM((96, 128), f32),
             pltpu.VMEM((2, 10, 20, 8, 128), f32),
             pltpu.VMEM((2, 6, 56, 8, 128), f32),

time: 31.3 us -> 31.3 us (level)
  no operation moved by 1% of the time
where the time goes in v6:
time: 31.3 us; the launch traced here: 31.1 us
  Pallas kernels  29 us (93%)
  other arithmetic  1.32 us (4%)
  between operations  0.66 us (2%)
    pallas_call x1, Pallas kernels, local(): pl.pallas_call(kernel, out_shape=(jax.ShapeDtypeStruct((320, 128), f32),...  29 us
    add x1, other arithmetic, local(): 0.75 * fine_start + fine.reshape(fine_start.shape)  0.7 us

profile of v6, /device:TPU:1, one launch (start us, length us, event | category | flops | bytes accessed | tf_op | source)
XLA Modules:
  0.0 31.1 jit_solution(14273968245935746788)
XLA Ops:
  0.6 0.0 copy-start
  0.6 29.0 %section.1 = (f32[320,128]{1,0:T(8,128)S(1)}, f32[80,64]{1,0:T(8,128)S(1)}) custom-call(f32[320,128]{1,0:T(8,128)} %bitcast.7, f32[192,128]{1,0:T(8,128)} %bitcast.8, f32[80,64]{1,0:T(8,128)} %bitcast.9, f32[3,9]{1,0:T(4,128)} %taps_hbm.1, s32[8]{0:T(128)} %owner_hbm.1), custom_call_target="tpu_custom_call" | custom-call | tf_op jit(solution)/shard_map/section/pallas_call | solution.py:625
  29.7 0.0 copy-done
  29.7 0.0 copy-start.1
  29.7 0.7 %multiply_add_fusion = f32[5,4,16,128]{3,2,1,0:T(8,128)} fusion(f32[5,4,16,128]{3,2,1,0:T(8,128)S(1)} %bitcast.5, f32[5,4,16,128]{3,2,1,0:T(8,128)S(1)} %copy-done), kind=kLoop, calls=%fused_computation | loop fusion | flops 81920 | bytes 491520 | tf_op jit(solution)/shard_map/add | solution.py:682
  30.4 0.1 copy-done.1
  30.5 0.6 %multiply_add_fusion.1 = f32[5,2,8,64]{3,2,1,0:T(8,128)} fusion(f32[5,2,8,64]{3,2,1,0:T(8,128)S(1)} %bitcast.6, f32[5,2,8,64]{3,2,1,0:T(8,128)S(1)} %copy-done.1), kind=kLoop, calls=%fused_computation.1 | loop fusion | flops 10240 | bytes 61440 | tf_op jit(solution)/shard_map/add | solution.py:683
Async XLA Ops:
  0.6 29.0 %copy-start = (f32[5,4,16,128]{3,2,1,0:T(8,128)S(1)}, f32[5,4,16,128]{3,2,1,0:T(8,128)}, u32[]{:S(2)}) copy-start(f32[5,4,16,128]{3,2,1,0:T(8,128)} %param.7) | copy-start | bytes 491524
  29.7 0.8 %copy-start.1 = (f32[5,2,8,64]{3,2,1,0:T(8,128)S(1)}, f32[5,2,8,64]{3,2,1,0:T(8,128)}, u32[]{:S(2)}) copy-start(f32[5,2,8,64]{3,2,1,0:T(8,128)} %param.10) | copy-start | bytes 61444
